TPU v7x, 32 devices: a whole 2x2x4 slice. The times are simulated.
32 devices in a mesh: seq: 8 (over y, x, core), head: 4 (over z).
Axes of the slice: x: 2, y: 2, z: 4, core: 2. Of those that a mesh axis runs over, the one named last changes fastest.
Arguments:
- queries: bfloat16 [8192, 8192], P('seq', 'head'), may hold values from -6 to 6
- key_rows: bfloat16 [8192, 8192], P('seq', 'head'), may hold values from -6 to 6
- value_rows: bfloat16 [8192, 8192], P('seq', 'head')
- log_decay: float32 [64, 8192], P('head', 'seq')
- doc_start: int32 [8192], P('seq'), may hold values from 0 to 1, as said below
- gate_input: bfloat16 [8192, 8192], P('seq', 'head'), may hold values from -6 to 6
- norm_gain: float32 [8192], P('head'), may hold values from 0.1 to 1.9
- out_grad: bfloat16 [8192, 8192], P('seq', 'head'), may hold values from -6 to 6
Outputs:
- gated: bfloat16 [8192, 8192], P('seq', 'head')
- gate_grad: bfloat16 [8192, 8192], P('seq', 'head')
- query_grad: bfloat16 [8192, 8192], P('seq', 'head')
- key_grad: bfloat16 [8192, 8192], P('seq', 'head')
- value_grad: bfloat16 [8192, 8192], P('seq', 'head')
Inputs may be any that keep to these rules, and one draw needn't show every extreme that they name: `doc_start`: only the first 512 and the last 512 tokens of the sequence can begin a document, and each of these two ranges holds at least one start; one document runs over all devices but the first and the last.
All inputs are finite; a program needn't handle non-finite values.
Results may differ from a plain program's by a relative error of at most 0.0062.
Values sent between devices are 32-bit elements; how exact they have to be, the bound alone decides.
No kernel may reach another device: no remote copies, remote signals or barrier semaphores. Data moves between devices by JAX's collectives and lax.ppermute only.
A program may use at most 128 MiB of HBM per device.

v0:
```python
import functools

import jax
import jax.numpy as jnp
from jax import lax
from jax.experimental import pallas as pl
from jax.experimental.pallas import tpu as pltpu
from jax.sharding import PartitionSpec as P

HEAD_TOTAL = 64
HD = 128
CHUNK = 256
GROUP = 2
WINDOWS = 4
WIDTH = HEAD_TOTAL * HD

epsilon = 1e-06
LOG2E = 1.4426950408889634

F32 = jnp.float32
BF16 = jnp.bfloat16
MIB = 1024 * 1024
NT = ((1,), (1,))


def dot(a, b, dims=((1,), (0,))):
    return lax.dot_general(a, b, (dims, ((), ())), preferred_element_type=F32)


def chunk_cumsum(x):
    lane = lax.broadcasted_iota(jnp.int32, x.shape, 1) % CHUNK
    shift = 1
    while shift < CHUNK:
        x = x + jnp.where(lane >= shift, pltpu.roll(x, shift, 1), 0.0)
        shift *= 2
    return x


def spans(chunks):
    return [slice(n * CHUNK, (n + 1) * CHUNK) for n in range(chunks)]


def head_span(head, count=1):
    return pl.ds(pl.multiple_of(head * HD, HD), count * HD)


def sigmoid(x):
    return 0.5 * jnp.tanh(0.5 * x) + 0.5


def spread(cols, lane):
    return jnp.broadcast_to(cols[:, lane : lane + 1], cols.shape)


def turned(cols_ref, lane):
    return pltpu.roll(cols_ref[...], (HD - lane) % HD, 1)


def column(row):
    return jnp.broadcast_to(row, (HD, row.shape[1])).T


def state_kernel(
    chunks, steps, lc_ref, doc_ref, k_hbm, v_hbm,
    crow_ref, enter_ref, leave_ref, rrow_ref, k_ref, v_ref, loc_ref, state_ref, pass_ref, sems,
):
    step = pl.program_id(0)

    def copies(at):
        here = head_span(at * GROUP, GROUP)
        return (
            pltpu.make_async_copy(k_hbm.at[:, here], k_ref.at[:, here], sems.at[0, at]),
            pltpu.make_async_copy(v_hbm.at[:, here], v_ref.at[:, here], sems.at[1, at]),
        )

    @pl.when(step == 0)
    def _():
        for at in range(steps):
            for copy in copies(at):
                copy.start()
        c = chunk_cumsum(lc_ref[...] * LOG2E)
        r = chunk_cumsum(jnp.broadcast_to(doc_ref[...].astype(F32), (8, doc_ref.shape[1])))
        crow_ref[...] = c
        rrow_ref[...] = r
        enter_ref[...] = jnp.where(r[0:1] == 0.0, jnp.exp2(c), 0.0)
        for span in spans(chunks):
            cn, rn = c[:, span], r[0:1, span]
            leave_ref[:, span] = jnp.where(rn == rn[:, -1:], jnp.exp2(cn[:, -1:] - cn), 0.0)

    for copy in copies(step):
        copy.wait()
    for g in range(GROUP):
        h = step * GROUP + g
        mine = head_span(h)
        state = None
        total = None
        for n, span in enumerate(spans(chunks)):
            keyed = (k_ref[span, mine].T.astype(F32) * leave_ref[pl.ds(h, 1), span]).astype(BF16)
            local = dot(keyed, v_ref[span, mine])
            loc_ref[h, n] = local
            passing = enter_ref[pl.ds(h, 1), span][:, CHUNK - 1 : CHUNK]
            state = local if state is None else passing * state + local
            total = passing if total is None else passing * total
        state_ref[h] = state
        pass_ref[pl.ds(h, 1), :] = jnp.broadcast_to(total, (1, HD))


def prepare_kernel(rrow_ref, crow_ref, enter_ref, mask_ref, cols_ref):
    sub = lax.broadcasted_iota(jnp.int32, (CHUNK, CHUNK), 0)
    lane = lax.broadcasted_iota(jnp.int32, (CHUNK, CHUNK), 1)
    spare = jnp.zeros((HD - 2 * crow_ref.shape[0], CHUNK), F32)
    for n, span in enumerate(spans(mask_ref.shape[0])):
        r_row = rrow_ref[0:1, span]
        r_col = jnp.concatenate([column(r_row)] * (CHUNK // HD), axis=1)
        mask_ref[n] = jnp.where((r_col == r_row) & (lane <= sub), 0.0, -jnp.inf)
        cols_ref[span, :] = jnp.concatenate([crow_ref[:, span], enter_ref[:, span], spare], axis=0).T


def decayed(scores, c_col, c_row, mask):
    top, low = slice(0, HD), slice(HD, CHUNK)
    row_blocks = []
    for rows, width in ((top, HD), (low, CHUNK)):
        col = c_col[rows]
        col = col if width == HD else jnp.concatenate([col] * (width // HD), axis=1)
        weight = jnp.exp2(col - c_row[:, :width] + mask[rows, :width])
        row_blocks.append((scores[rows, :width] * weight).astype(BF16))
    row_blocks[0] = jnp.concatenate([row_blocks[0], jnp.zeros((HD, CHUNK - HD), BF16)], axis=1)
    return jnp.concatenate(row_blocks, axis=0)


def inside_kernel(
    chunks, first, steps, crow_ref, cols_ref, mask_ref, k_ref, v_ref, gain_ref, q_hbm, gate_ref,
    grad_ref, *refs,
):
    attn_ref, gnorm_ref, q_ref, turned_q_ref, probs_ref, sems = refs[-6:]
    step = pl.program_id(0)

    def copy(at):
        here = head_span(first + at)
        return pltpu.make_async_copy(q_hbm.at[:, here], q_ref.at[:, here], sems.at[at])

    @pl.when(step == 0)
    def _():
        for at in range(steps):
            copy(at).start()

    cols_now = turned(cols_ref, first + step)
    copy(step).wait()
    for g in range(1):
        h = first + step
        cols = slice(g * HD, (g + 1) * HD)
        mine = head_span(h)
        for n, span in enumerate(spans(chunks)):
            q = q_ref[span, mine]
            scores = dot(q, k_ref[span, mine], NT)
            c_row = crow_ref[pl.ds(h, 1), span]
            probs = decayed(scores, spread(cols_now[span], g), c_row, mask_ref.at[n])
            probs_ref[g, n] = probs
            attn_ref[span, mine] = dot(probs, v_ref[span, mine])
            turned_q_ref[h, :, span] = q.T
            sig = sigmoid(gate_ref[span, cols].astype(F32))
            gnorm = grad_ref[span, cols].astype(F32) * sig * gain_ref[0:1, cols]
            gnorm_ref[span, mine] = gnorm.astype(BF16)


def outside_kernel(chunks, entering, inputs, cols_ref, enter_ref, q_ref, gnorm_ref, loc_ref, *refs):
    in_refs = refs[:inputs]
    inside_ref, attn_ref, held_ref, sums_ref, sq_ref, inner_ref = refs[inputs:]
    step = pl.program_id(0)

    @pl.when(step == 0)
    def _():
        sq_ref[...] = jnp.zeros_like(sq_ref)
        inner_ref[...] = jnp.zeros_like(inner_ref)

    heads = [step * GROUP + g for g in range(GROUP)]
    cols_now = turned(cols_ref, enter_ref.shape[0] + step * GROUP)
    carries = [entering(in_refs, h) for h in heads]
    for n, span in enumerate(spans(chunks)):
        squares = sq_ref[span, :]
        inners = inner_ref[span, :]
        for g, h in enumerate(heads):
            mine = head_span(h)
            held = carries[g].astype(BF16)
            held_ref[h, n] = held
            enter = spread(cols_now[span], g)
            attn = inside_ref[span, mine] + enter * dot(q_ref[span, mine], held)
            attn_ref[span, mine] = attn
            squares = squares + attn * attn
            inners = inners + gnorm_ref[span, mine].astype(F32) * attn
            if n + 1 < chunks:
                passing = enter_ref[pl.ds(h, 1), span][:, CHUNK - 1 : CHUNK]
                carries[g] = passing * carries[g] + loc_ref[h, n]
        sq_ref[span, :] = squares
        inner_ref[span, :] = inners

    @pl.when(step == pl.num_programs(0) - 1)
    def _():
        sums_ref[0:1, :] = jnp.sum(sq_ref[...].T, axis=0, keepdims=True)
        sums_ref[1:2, :] = jnp.sum(inner_ref[...].T, axis=0, keepdims=True)


def grad_kernel(chunks, parts, enter_ref, *refs):
    turned_q_ref, gnorm_ref, attn_ref = refs[parts : parts + 3]
    agrad_ref, turned_ref, bloc_ref, back_ref, alpha_ref, beta_ref = refs[parts + 3 :]
    step = pl.program_id(0)

    @pl.when(step == 0)
    def _():
        sums = refs[0][...]
        for ref in refs[1:parts]:
            sums = sums + ref[...]
        inverse = lax.rsqrt(sums[0:1] / WIDTH + epsilon)
        alpha_ref[...] = column(inverse)
        beta_ref[...] = column(inverse * inverse * inverse * sums[1:2] / WIDTH)

    for g in range(GROUP):
        h = step * GROUP + g
        mine = head_span(h)
        back = None
        for n, span in reversed(list(enumerate(spans(chunks)))):
            enter = enter_ref[pl.ds(h, 1), span]
            gnorm = gnorm_ref[span, mine].astype(F32)
            agrad = alpha_ref[span, :] * gnorm - attn_ref[span, mine] * beta_ref[span, :]
            agrad = agrad.astype(BF16)
            agrad_ref[span, mine] = agrad
            turned_ref[h, :, span] = agrad.T
            qkeyed = (turned_q_ref[h, :, span].astype(F32) * enter).astype(BF16)
            local = dot(qkeyed, agrad)
            bloc_ref[h, n] = local
            back = local if back is None else local + enter[:, CHUNK - 1 : CHUNK] * back
        back_ref[h] = back


def inner_grad_kernel(
    chunks, first, crow_ref, alpha_ref, cols_ref, mask_ref, k_ref, v_ref, attn_ref, held_ref,
    agrad_ref, turned_q_ref, turned_agrad_ref, gain_ref, gate_ref, grad_ref, probs_ref, *refs,
):
    dk_ref, dv_ref, dq_ref, gated_ref, ggate_ref = refs[-5:]
    step = pl.program_id(0)
    cols_now = turned(cols_ref, first + step)
    for g in range(1):
        h = first + step
        cols = slice(g * HD, (g + 1) * HD)
        mine = head_span(h)
        for n, span in enumerate(spans(chunks)):
            k, v, agrad = k_ref[span, mine], v_ref[span, mine], agrad_ref[span, mine]
            both = dot(agrad, jnp.concatenate([v, held_ref[h, n]], axis=0), NT)
            c_row = crow_ref[pl.ds(h, 1), span]
            dscore = decayed(both[:, :CHUNK], spread(cols_now[span], g), c_row, mask_ref.at[n])
            enter = spread(cols_now[span], crow_ref.shape[0] + g)
            dq_ref[span, cols] = (dot(dscore, k) + enter * both[:, CHUNK:]).astype(BF16)
            dv_ref[h, :, span] = dot(turned_agrad_ref[h, :, span], probs_ref[g, n]).astype(BF16)
            dk_ref[h, :, span] = dot(turned_q_ref[h, :, span], dscore).astype(BF16)
            normed = attn_ref[span, mine] * alpha_ref[span, :] * gain_ref[0:1, cols]
            sig = sigmoid(gate_ref[span, cols].astype(F32))
            gated = normed * sig
            gated_ref[span, cols] = gated.astype(BF16)
            ggate = grad_ref[span, cols].astype(F32) * gated * (1.0 - sig)
            ggate_ref[span, cols] = ggate.astype(BF16)


def outer_grad_kernel(chunks, entering, inputs, enter_ref, leave_ref, k_ref, v_ref, *refs):
    in_refs = refs[:inputs]
    dkin_ref, dvin_ref, bloc_ref, dk_ref, dv_ref = refs[inputs:]
    step = pl.program_id(0)
    for g in range(GROUP):
        h = step * GROUP + g
        cols = slice(g * HD, (g + 1) * HD)
        mine = head_span(h)
        carry = entering(in_refs, h)
        for n, span in reversed(list(enumerate(spans(chunks)))):
            leave = leave_ref[pl.ds(h, 1), span]
            back = carry.astype(BF16)
            dk = dkin_ref[h, :, span].astype(F32) + leave * dot(back, v_ref[span, mine], NT)
            dv = dvin_ref[h, :, span].astype(F32) + leave * dot(back.T, k_ref[span, mine], NT)
            dk_ref[span, cols] = dk.astype(BF16).T
            dv_ref[span, cols] = dv.astype(BF16).T
            if n > 0:
                passing = enter_ref[pl.ds(h, 1), span][:, CHUNK - 1 : CHUNK]
                carry = bloc_ref[h, n] + passing * carry


def hbm(x):
    return pltpu.with_memory_space_constraint(x, pltpu.HBM)


def kept(*arrays):
    spec = pl.BlockSpec(memory_space=pltpu.VMEM)
    return [(pltpu.with_memory_space_constraint(x, pltpu.VMEM), spec) for x in arrays]


def keep(dims, dtype):
    return pltpu.VMEM(dims, dtype), pl.BlockSpec(memory_space=pltpu.VMEM)


def add_kernel(a_ref, b_ref, out_ref):
    out_ref[...] = a_ref[...] + b_ref[...]


def call(kernel, grid, ins, outs, scratch=(), aliases=None, room=8, flops=0, moved=0, exps=0):
    return pl.pallas_call(
        kernel,
        grid=grid,
        in_specs=[spec for _, spec in ins],
        out_specs=[spec for _, spec in outs],
        out_shape=[shape for shape, _ in outs],
        scratch_shapes=list(scratch),
        input_output_aliases=aliases or {},
        compiler_params=pltpu.CompilerParams(
            dimension_semantics=("arbitrary",) * len(grid), vmem_limit_bytes=room * MIB
        ),
        cost_estimate=pl.CostEstimate(flops=flops, bytes_accessed=moved, transcendentals=exps),
    )(*[x for x, _ in ins])


def after(x, *others):
    return lax.optimization_barrier((x, *others))[0]


def across(x, flips, devices=8):
    return lax.ppermute(x, "seq", [(i, i ^ flips) for i in range(devices)])


def place(reverse):
    index = lax.axis_index("seq")
    index = 7 - index if reverse else index
    return lax.rem(index, 2), lax.rem(lax.div(index, 2), 2), lax.div(index, 4)


def pair_kernel(reverse, state_ref, other_ref, pass_ref, beside_ref, x_ref, y_ref, chip_ref):
    core, _, _ = place(reverse)
    quarter = x_ref.shape[0]
    chip_ref[...] = pass_ref[...] * beside_ref[...]
    for i in range(quarter):
        for at, out_ref in ((i, x_ref), (quarter + i, y_ref)):
            h = core * 2 * quarter + at
            mine, other = state_ref[h], other_ref[h]

            @pl.when(core == 0)
            def _():
                out_ref[i] = beside_ref[pl.ds(h, 1), :] * mine + other

            @pl.when(core == 1)
            def _():
                out_ref[i] = pass_ref[pl.ds(h, 1), :] * other + mine


def row_kernel(
    reverse, to_x_ref, to_y_ref, from_x_ref, from_y_ref, chip_ref, side_ref, far_ref,
    row_ref, sent_ref,
):
    core, x, y = place(reverse)
    quarter = row_ref.shape[0]
    for i in range(quarter):
        h = core * 2 * quarter + i
        hy = h + quarter

        @pl.when(x == 0)
        def _():
            row_ref[i] = side_ref[pl.ds(h, 1), :] * to_x_ref[i] + from_x_ref[i]

        @pl.when(x == 1)
        def _():
            row_ref[i] = chip_ref[pl.ds(h, 1), :] * from_x_ref[i] + to_x_ref[i]

        @pl.when(y == 0)
        def _():
            sent_ref[i] = to_y_ref[i]

        @pl.when((y == 1) & (x == 0))
        def _():
            far = far_ref[pl.ds(hy, 1), :] * from_y_ref[i]
            sent_ref[i] = chip_ref[pl.ds(hy, 1), :] * far + to_y_ref[i]

        @pl.when((y == 1) & (x == 1))
        def _():
            sent_ref[i] = from_y_ref[i]


def ahead_kernel(
    reverse, from_x_ref, from_y_ref, row_ref, sent_ref, side_ref, far_ref, out_ref,
):
    core, x, y = place(reverse)
    quarter = row_ref.shape[0]
    for i in range(quarter):
        h = core * 2 * quarter + i
        hy = h + quarter

        @pl.when((y == 0) & (x == 0))
        def _():
            out_ref[i] = jnp.zeros_like(out_ref[i])
            out_ref[quarter + i] = jnp.zeros_like(out_ref[i])

        @pl.when((y == 0) & (x == 1))
        def _():
            out_ref[i] = from_x_ref[i]
            out_ref[quarter + i] = sent_ref[i]

        @pl.when((y == 1) & (x == 0))
        def _():
            out_ref[i] = row_ref[i]
            out_ref[quarter + i] = far_ref[pl.ds(hy, 1), :] * from_y_ref[i] + sent_ref[i]

        @pl.when((y == 1) & (x == 1))
        def _():
            out_ref[i] = side_ref[pl.ds(h, 1), :] * row_ref[i] + from_x_ref[i]
            out_ref[quarter + i] = side_ref[pl.ds(hy, 1), :] * from_y_ref[i] + sent_ref[i]


def cube_entering(reverse, refs, h):
    ahead_ref, beside_ref, other_ref, beside_pass_ref = refs
    core, _, _ = place(reverse)
    half = ahead_ref.shape[0]
    at = lax.rem(h, half)
    chip = jnp.where(lax.div(h, half) == core, ahead_ref[at], beside_ref[at])
    through = beside_pass_ref[pl.ds(h, 1), :] * chip + other_ref[h]
    return jnp.where(core == 0, chip, through)


def plain_entering(refs, h):
    return refs[0][h]


def cube_scan(state, own_pass, passes, fill, reverse):
    heads = state.shape[0]
    quarter = heads // 4
    part = keep((quarter, HD, HD), F32)

    other = across(state, 1)
    beside_pass = passes[0] if passes else across(own_pass, 1)
    other, beside_pass = lax.optimization_barrier((other, beside_pass, fill(0, state)))[:2]
    to_x, to_y, chip_pass = call(
        functools.partial(pair_kernel, reverse), (),
        kept(state, other, own_pass, beside_pass), [part, part, keep((heads, HD), F32)], room=2,
    )

    from_x, from_y = across(to_x, 2), across(to_y, 4)
    x_pass, far_pass = passes[1:] if passes else (across(chip_pass, 2), across(chip_pass, 6))
    from_x, from_y, x_pass, far_pass = lax.optimization_barrier(
        (from_x, from_y, x_pass, far_pass, fill(1, to_y))
    )[:4]
    row, sent = call(
        functools.partial(row_kernel, reverse), (),
        kept(to_x, to_y, from_x, from_y, chip_pass, x_pass, far_pass), [part, part], room=2,
    )

    row_in, sent_in = across(row, 4), across(sent, 2)
    row_in, sent_in = lax.optimization_barrier((row_in, sent_in, fill(2, sent)))[:2]
    (ahead,) = call(
        functools.partial(ahead_kernel, reverse), (),
        kept(from_x, from_y, row_in, sent_in, x_pass, far_pass),
        [keep((2 * quarter, HD, HD), F32)], room=2,
    )

    beside = across(ahead, 1)
    beside = after(beside, fill(3, ahead))
    entering = functools.partial(cube_entering, reverse)
    return entering, (ahead, beside, other, beside_pass), (beside_pass, x_pass, far_pass)


def doubling_scan(state, own_pass, fill, reverse):
    devices = lax.axis_size("seq")
    index = lax.axis_index("seq")
    passes = lax.all_gather(own_pass, "seq")
    if reverse:
        passes = passes[::-1]
        index = devices - 1 - index
    route = lambda hop: [
        (i, i - hop if reverse else i + hop)
        for i in range(devices)
        if 0 <= (i - hop if reverse else i + hop) < devices
    ]
    for window in range(WINDOWS):
        state = after(state, fill(window, state))
    hop = 1
    while hop < devices:
        factor = lax.dynamic_index_in_dim(passes, index, 0, False)
        state = factor[:, None, :] * lax.ppermute(state, "seq", route(hop)) + state
        before = jnp.concatenate([jnp.zeros_like(passes[:hop]), passes[:-hop]], axis=0)
        passes = passes * before
        hop *= 2
    return lax.ppermute(state, "seq", route(1))


def scan_devices(state, own_pass, passes, fill, reverse):
    if lax.axis_size("seq") == 8 and state.shape[0] % 4 == 0:
        return cube_scan(state, own_pass, passes, fill, reverse)
    return plain_entering, (doubling_scan(state, own_pass, fill, reverse),), None


def body(queries, key_rows, value_rows, log_decay, doc_start, gate_input, norm_gain, out_grad):
    rows, cols = queries.shape
    heads = cols // HD
    chunks = rows // CHUNK
    parts = lax.axis_size("head")
    grid = (heads // GROUP,)
    share = heads // WINDOWS
    big = rows * cols * 2
    tile = 2 * rows * CHUNK * cols
    small = 2 * rows * HD * cols

    whole = lambda *dims: pl.BlockSpec(dims, lambda i: (0,) * len(dims))
    anywhere = pl.BlockSpec(memory_space=pl.ANY)

    def wide(base=0, group=1):
        return pl.BlockSpec((rows, group * HD), lambda i: (0, i + base // group))

    def gain_spec(base=0):
        return pl.BlockSpec((1, HD), lambda i: (0, i + base))

    probs_spec = pl.BlockSpec((1, chunks, CHUNK, CHUNK), lambda i: (i, 0, 0, 0))
    by_head = (heads, HD, rows)
    local_dims = (heads, chunks, HD, HD)
    wide_shape = pltpu.HBM((rows, cols), BF16)
    queries, key_rows, value_rows, gate_input, out_grad = map(
        hbm, (queries, key_rows, value_rows, gate_input, out_grad)
    )
    doc_row = doc_start.reshape(1, rows)
    gain_row = norm_gain.reshape(1, cols)

    by_token = (rows, cols)
    steps = heads // GROUP
    crow, enter, leave, rrow, keys, values, local, state, own_pass = call(
        functools.partial(state_kernel, chunks, steps),
        grid,
        [
            (hbm(log_decay), whole(heads, rows)), (hbm(doc_row), whole(1, rows)),
            (key_rows, anywhere), (value_rows, anywhere),
        ],
        [keep((heads, rows), F32)] * 3
        + [
            keep((8, rows), F32), keep(by_token, BF16), keep(by_token, BF16),
            keep(local_dims, F32), keep((heads, HD, HD), F32), keep((heads, HD), F32),
        ],
        [pltpu.SemaphoreType.DMA((2, steps))],
        flops=small, moved=2 * big,
    )

    ready = []
    made = []
    probs = []

    def fill_forward(window, tie):
        base = window * share
        if not ready:
            ready[:] = call(
                prepare_kernel, (), kept(after(rrow, tie), crow, enter),
                [keep((chunks, CHUNK, CHUNK), F32), keep((rows, HD), F32)],
                flops=8 * rows * CHUNK,
            )
        mask, columns = ready
        ins = kept(after(crow, tie), columns, mask, keys, values) + [
            (hbm(gain_row), gain_spec(base)), (queries, anywhere), (gate_input, wide(base)),
            (out_grad, wide(base)),
        ]
        aliases = {len(ins) + i: i for i in range(len(made))}
        ins += kept(*made)
        *made[:], fresh = call(
            functools.partial(inside_kernel, chunks, base, share),
            (share,),
            ins,
            [
                keep(by_token, F32), keep(by_token, BF16), keep(by_token, BF16),
                keep(by_head, BF16),
                (pltpu.HBM((share, chunks, CHUNK, CHUNK), BF16), probs_spec),
            ],
            [pltpu.SemaphoreType.DMA((share,))],
            aliases=aliases, room=6,
            flops=2 * tile // WINDOWS, moved=5 * big // WINDOWS,
            exps=rows * (CHUNK + HD) * heads // WINDOWS,
        )
        probs.append(fresh)
        return fresh

    entering, incoming, passes = scan_devices(state, own_pass, None, fill_forward, False)
    mask, columns = ready
    inside, gnorm, kept_q, turned_q = made
    tall = pltpu.VMEM((rows, HD), F32)

    attn, held, sums = call(
        functools.partial(outside_kernel, chunks, entering, len(incoming)),
        grid,
        kept(columns, enter, kept_q, gnorm, local, *incoming, inside),
        [keep(by_token, F32), keep(local_dims, BF16), keep((2, rows), F32)],
        [tall, tall],
        {5 + len(incoming): 0},
        flops=small, moved=big,
    )

    apart = 1
    while apart < parts // 2:
        other_sums = lax.ppermute(sums, "head", [(i, i ^ apart) for i in range(parts)])
        (sums,) = call(add_kernel, (), kept(sums, other_sums), [keep((2, rows), F32)], room=2)
        apart *= 2
    other_sums = lax.ppermute(sums, "head", [(i, i ^ apart) for i in range(parts)])

    agrad, turned_agrad, bloc, back, alpha, _ = call(
        functools.partial(grad_kernel, chunks, 2),
        grid,
        kept(enter, sums, other_sums, turned_q, gnorm, attn),
        [
            keep(by_token, BF16), keep(by_head, BF16), keep(local_dims, F32),
            keep((heads, HD, HD), F32), keep((rows, HD), F32), keep((rows, HD), F32),
        ],
        flops=small, moved=big,
    )

    inner = [turned_q, turned_agrad]
    outs = []

    def fill_backward(window, tie):
        base = window * share
        ins = kept(
            after(crow, tie), alpha, columns, mask, keys, values, attn, held, agrad, *inner
        )
        aliases = {len(ins) - 2: 0, len(ins) - 1: 1}
        ins += [
            (hbm(gain_row), gain_spec(base)), (gate_input, wide(base)), (out_grad, wide(base)),
            (hbm(probs[window]), probs_spec),
        ]
        aliases.update({len(ins) + i: 2 + i for i in range(len(outs))})
        ins += [(hbm(x), anywhere) for x in outs]
        inner[0], inner[1], *outs[:] = call(
            functools.partial(inner_grad_kernel, chunks, base),
            (share,),
            ins,
            [keep(by_head, BF16)] * 2 + [(wide_shape, wide(base))] * 3,
            aliases=aliases, room=6,
            flops=(4 * tile + small) // WINDOWS, moved=7 * big // WINDOWS,
            exps=rows * (CHUNK + HD) * heads // WINDOWS,
        )
        return outs[0]

    entering, outgoing, _ = scan_devices(back, own_pass, passes, fill_backward, True)
    dq, gated, gate_grad = outs

    dk, dv = call(
        functools.partial(outer_grad_kernel, chunks, entering, len(outgoing)),
        grid,
        kept(enter, leave, keys, values, *outgoing, *inner, bloc),
        [(wide_shape, wide(0, GROUP))] * 2,
        flops=2 * small, moved=2 * big,
    )
    return (gated, gate_grad, dq, dk, dv)


def solution(mesh):
    in_specs = (
        P("seq", "head"),
        P("seq", "head"),
        P("seq", "head"),
        P("head", "seq"),
        P("seq"),
        P("seq", "head"),
        P("head"),
        P("seq", "head"),
    )
    out_specs = (P("seq", "head"),) * 5
    return jax.shard_map(body, mesh=mesh, in_specs=in_specs, out_specs=out_specs, check_vma=False)
```

profile of v0, /device:TPU:0, one launch (start us, length us, event | category | flops | bytes accessed | tf_op | source)
XLA Modules:
  0.0 108.1 jit_solution(14038007132833651360)
XLA Ops:
  0.6 6.3 %shard_map.119 = (f32[16,1024]{1,0:T(8,128)S(1)}, f32[16,1024]{1,0:T(8,128)S(1)}, f32[16,1024]{1,0:T(8,128)S(1)}, f32[8,1024]{1,0:T(8,128)S(1)}, bf16[1024,2048]...) custom-call(f32[16,1024]{1,0:T(8,128)} %lc_ref.1, ...), custom_call_target="tpu_custom_call" | custom-call | flops 536870912 | bytes 8388608 | tf_op jit(solution)/shard_map/pallas_call | solution.py:302
  7.8 6.9 %shard_map.121 = (f32[1024,2048]{1,0:T(8,128)S(1)}, bf16[1024,2048]{1,0:T(8,128)(2,1)S(1)}, bf16[1024,2048]{1,0:T(8,128)(2,1)S(1)}, bf16[16,128,1024]{2,1,0:T(8,128)(2,1)S(1)}, bf16[4,4,256,256]{3,2,1,0:T(8,128)(2,1)}) custom-call(f32[16,1024]{1,0:T(8,128)S(1)} %get-tuple-element.186.crow_ref, f32[1024,128]{1,0:T(8,128)S(1)} %get-tuple-element.108.cols_ref, ...), custom_call_target="tpu_custom_call" | custom-call | flops 536870912 | bytes 5242880 | tf_op jit(solution)/shard_map/pallas_call | solution.py:302
  15.0 3.0 %collective-permute-start.2 = (f32[4,128,128]{2,1,0:T(8,128)S(1)}, f32[4,128,128]{2,1,0:T(8,128)S(1)}, u32[]{:S(2)}, u32[]{:S(2)}) collective-permute-start(f32[4,128,128]{2,1,0:T(8,128)S(1)} %get-tuple-element.117.to_x_ref), channel_id=1, source_target_pairs={{0,8},{4,12},{8,0},{12,4},{16,24},{20,28},{24,16},{28,20},{1,9},{5... | collective-permute-start | bytes 786440 | tf_op jit(solution)/shard_map/ppermute | solution.py:322
  17.9 1.5 %collective-permute-start.3 = (f32[4,128,128]{2,1,0:T(8,128)S(1)}, f32[4,128,128]{2,1,0:T(8,128)S(1)}, u32[]{:S(2)}, u32[]{:S(2)}) collective-permute-start(f32[4,128,128]{2,1,0:T(8,128)S(1)} %get-tuple-element.118.to_y_ref), channel_id=1, source_target_pairs={{0,16},{4,20},{8,24},{12,28},{16,0},{20,4},{24,8},{28,12},{1,17},{... | collective-permute-start | bytes 786440 | tf_op jit(solution)/shard_map/ppermute | solution.py:322
  19.5 1.9 %collective-permute-start.4 = (f32[16,128]{1,0:T(8,128)S(1)}, f32[16,128]{1,0:T(8,128)S(1)}, u32[]{:S(2)}, u32[]{:S(2)}) collective-permute-start(f32[16,128]{1,0:T(8,128)S(1)} %get-tuple-element.119.chip_ref), channel_id=1, source_target_pairs={{0,8},{4,12},{8,0},{12,4},{16,24},{20,28},{24,16},{28,20},{1,9},{5... | collective-permute-start | bytes 24584 | tf_op jit(solution)/shard_map/ppermute | solution.py:322
  21.4 6.9 %shard_map.123 = (f32[1024,2048]{1,0:T(8,128)S(1)}, bf16[1024,2048]{1,0:T(8,128)(2,1)S(1)}, bf16[1024,2048]{1,0:T(8,128)(2,1)S(1)}, bf16[16,128,1024]{2,1,0:T(8,128)(2,1)S(1)}, bf16[4,4,256,256]{3,2,1,0:T(8,128)(2,1)}) custom-call(f32[16,1024]{1,0:T(8,128)S(1)} %get-tuple-element.186.crow_, ...), custom_call_target="tpu_custom_call", output_to_operand_aliasing={{0}: (9, {}), {1}: (10, {}), {2}: (11, {}), {3}: (12, {})} | custom-call | flops 536870912 | bytes 5242880 | tf_op jit(solution)/shard_map/pallas_call | solution.py:302
  28.6 1.6 %collective-permute-start.6 = (f32[4,128,128]{2,1,0:T(8,128)S(1)}, f32[4,128,128]{2,1,0:T(8,128)S(1)}, u32[]{:S(2)}, u32[]{:S(2)}) collective-permute-start(f32[4,128,128]{2,1,0:T(8,128)S(1)} %get-tuple-element.130), channel_id=1, source_target_pairs={{0,16},{4,20},{8,24},{12,28},{16,0},{20,4},{24,8},{28,12},{1,17},{... | collective-permute-start | bytes 786440 | tf_op jit(solution)/shard_map/ppermute | solution.py:322
  30.7 6.9 %shard_map.125 = (f32[1024,2048]{1,0:T(8,128)S(1)}, bf16[1024,2048]{1,0:T(8,128)(2,1)S(1)}, bf16[1024,2048]{1,0:T(8,128)(2,1)S(1)}, bf16[16,128,1024]{2,1,0:T(8,128)(2,1)S(1)}, bf16[4,4,256,256]{3,2,1,0:T(8,128)(2,1)}) custom-call(f32[16,1024]{1,0:T(8,128)S(1)} %get-tuple-element.186.crow_, ...), custom_call_target="tpu_custom_call", output_to_operand_aliasing={{0}: (9, {}), {1}: (10, {}), {2}: (11, {}), {3}: (12, {})} | custom-call | flops 536870912 | bytes 5242880 | tf_op jit(solution)/shard_map/pallas_call | solution.py:302
  37.8 7.0 %shard_map.127 = (f32[1024,2048]{1,0:T(8,128)S(1)}, bf16[1024,2048]{1,0:T(8,128)(2,1)S(1)}, bf16[1024,2048]{1,0:T(8,128)(2,1)S(1)}, bf16[16,128,1024]{2,1,0:T(8,128)(2,1)S(1)}, bf16[4,4,256,256]{3,2,1,0:T(8,128)(2,1)}) custom-call(f32[16,1024]{1,0:T(8,128)S(1)} %get-tuple-element.186.crow_, ...), custom_call_target="tpu_custom_call", output_to_operand_aliasing={{0}: (9, {}), {1}: (10, {}), {2}: (11, {}), {3}: (12, {})} | custom-call | flops 536870912 | bytes 5242880 | tf_op jit(solution)/shard_map/pallas_call | solution.py:302
  44.8 7.8 %shard_map.128 = (f32[1024,2048]{1,0:T(8,128)S(1)}, bf16[16,4,128,128]{3,2,1,0:T(8,128)(2,1)S(1)}, f32[2,1024]{1,0:T(2,128)S(1)}) custom-call(f32[1024,128]{1,0:T(8,128)S(1)} %get-tuple-element.108.cols_ref, f32[16,1024]{1,0:T(8,128)S(1)} %get-tuple-element.104.enter_ref, ...), custom_call_target="tpu_custom_call", output_to_operand_aliasing={{0}: (9, {})} | custom-call | flops 536870912 | bytes 4194304 | tf_op jit(solution)/shard_map/pallas_call | solution.py:302
  52.5 1.6 %collective-permute-start.9 = (f32[2,1024]{1,0:T(2,128)S(1)}, f32[2,1024]{1,0:T(2,128)S(1)}, u32[]{:S(2)}, u32[]{:S(2)}) collective-permute-start(f32[2,1024]{1,0:T(2,128)S(1)} %get-tuple-element.151.a_ref), channel_id=1, source_target_pairs={{0,1},{1,0},{2,3},{3,2},{4,5},{5,4},{6,7},{7,6},{8,9},{9,8},{10,11... | collective-permute-start | bytes 24584 | tf_op jit(solution)/shard_map/ppermute | solution.py:593
  54.2 2.1 %collective-permute-done.9.b_ref = f32[2,1024]{1,0:T(2,128)S(1)} collective-permute-done((f32[2,1024]{1,0:T(2,128)S(1)}, f32[2,1024]{1,0:T(2,128)S(1)}, u32[]{:S(2)}, u32[]{:S(2)}) %collective-permute-start.9) | collective-permute-done | bytes 8224 | tf_op jit(solution)/shard_map/ppermute | solution.py:593
  56.3 2.6 %collective-permute-start.10 = (f32[2,1024]{1,0:T(2,128)S(1)}, f32[2,1024]{1,0:T(2,128)S(1)}, u32[]{:S(2)}, u32[]{:S(2)}) collective-permute-start(f32[2,1024]{1,0:T(2,128)S(1)} %shard_map.129.refs_0_), channel_id=1, source_target_pairs={{0,2},{1,3},{2,0},{3,1},{4,6},{5,7},{6,4},{7,5},{8,10},{9,11},{10,... | collective-permute-start | bytes 24584 | tf_op jit(solution)/shard_map/ppermute | solution.py:596
  58.9 2.0 %collective-permute-done.10.refs_1_ = f32[2,1024]{1,0:T(2,128)S(1)} collective-permute-done((f32[2,1024]{1,0:T(2,128)S(1)}, f32[2,1024]{1,0:T(2,128)S(1)}, u32[]{:S(2)}, u32[]{:S(2)}) %collective-permute-start.10) | collective-permute-done | bytes 8224 | tf_op jit(solution)/shard_map/ppermute | solution.py:596
  60.8 5.6 %shard_map.130 = (bf16[1024,2048]{1,0:T(8,128)(2,1)S(1)}, bf16[16,128,1024]{2,1,0:T(8,128)(2,1)S(1)}, f32[16,4,128,128]{3,2,1,0:T(8,128)S(1)}, f32[16,128,128]{2...) custom-call(f32[16,1024]{1,0:T(8,128)S(1)} %get-tuple-element.104.enter_ref, ...), custom_call_target="tpu_custom_call" | custom-call | flops 536870912 | bytes 4194304 | tf_op jit(solution)/shard_map/pallas_call | solution.py:302
  66.5 7.2 %shard_map.131 = (bf16[16,128,1024]{2,1,0:T(8,128)(2,1)S(1)}, bf16[16,128,1024]{2,1,0:T(8,128)(2,1)S(1)}, bf16[1024,2048]{1,0:T(8,128)(2,1)}, bf16[1024,2048]{1,0:T(8,128)(2,1)}, bf16[1024,2048]{1,0:T(8,128)(2,1)}) custom-call(f32[16,1024]{1,0:T(8,128)S(1)} %get-tuple-element.186.crow_ref, ...), custom_call_target="tpu_custom_call", output_to_operand_aliasing={{0}: (9, {}), {1}: (10, {})} | custom-call | flops 1207959552 | bytes 7340032 | tf_op jit(solution)/shard_map/pallas_call | solution.py:302
  73.8 1.6 %collective-permute-start.12 = (f32[4,128,128]{2,1,0:T(8,128)S(1)}, f32[4,128,128]{2,1,0:T(8,128)S(1)}, u32[]{:S(2)}, u32[]{:S(2)}) collective-permute-start(f32[4,128,128]{2,1,0:T(8,128)S(1)} %get-tuple-element.163.to_x_ref), channel_id=1, source_target_pairs={{0,8},{4,12},{8,0},{12,4},{16,24},{20,28},{24,16},{28,20},{1,9},{5... | collective-permute-start | bytes 786440 | tf_op jit(solution)/shard_map/ppermute | solution.py:322
  75.9 7.2 %shard_map.133 = (bf16[16,128,1024]{2,1,0:T(8,128)(2,1)S(1)}, bf16[16,128,1024]{2,1,0:T(8,128)(2,1)S(1)}, bf16[1024,2048]{1,0:T(8,128)(2,1)}, bf16[1024,2048]{1,0:T(8,128)(2,1)}, bf16[1024,2048]{1,0:T(8,128)(2,1)}) custom-call(f32[16,1024]{1,0:T(8,128)S(1)} %get-tuple-element.186.crow_, ...), custom_call_target="tpu_custom_call", output_to_operand_aliasing={{0}: (9, {}), {1}: (10, {}), {2}: (15, {}), {3}: (16, {}), ... | custom-call | flops 1207959552 | bytes 7340032 | tf_op jit(solution)/shard_map/pallas_call | solution.py:302
  83.1 0.7 collective-permute-done.13.from_y_ref
  84.1 0.9 collective-permute-start.14
  85.0 0.5 collective-permute-start.15
  85.5 7.2 %shard_map.135 = (bf16[16,128,1024]{2,1,0:T(8,128)(2,1)S(1)}, bf16[16,128,1024]{2,1,0:T(8,128)(2,1)S(1)}, bf16[1024,2048]{1,0:T(8,128)(2,1)}, bf16[1024,2048]{1,0:T(8,128)(2,1)}, bf16[1024,2048]{1,0:T(8,128)(2,1)}) custom-call(f32[16,1024]{1,0:T(8,128)S(1)} %get-tuple-element.186.crow_, ...), custom_call_target="tpu_custom_call", output_to_operand_aliasing={{0}: (9, {}), {1}: (10, {}), {2}: (15, {}), {3}: (16, {}), ... | custom-call | flops 1207959552 | bytes 7340032 | tf_op jit(solution)/shard_map/pallas_call | solution.py:302
  93.1 7.3 %shard_map.137 = (bf16[16,128,1024]{2,1,0:T(8,128)(2,1)S(1)}, bf16[16,128,1024]{2,1,0:T(8,128)(2,1)S(1)}, bf16[1024,2048]{1,0:T(8,128)(2,1)}, bf16[1024,2048]{1,0:T(8,128)(2,1)}, bf16[1024,2048]{1,0:T(8,128)(2,1)}) custom-call(f32[16,1024]{1,0:T(8,128)S(1)} %get-tuple-element.186.crow_, ...), custom_call_target="tpu_custom_call", output_to_operand_aliasing={{0}: (9, {}), {1}: (10, {}), {2}: (15, {}), {3}: (16, {}), ... | custom-call | flops 1207959552 | bytes 7340032 | tf_op jit(solution)/shard_map/pallas_call | solution.py:302
  100.3 7.7 %shard_map.138 = (bf16[1024,2048]{1,0:T(8,128)(2,1)}, bf16[1024,2048]{1,0:T(8,128)(2,1)}) custom-call(f32[16,1024]{1,0:T(8,128)S(1)} %get-tuple-element.104.enter_ref, f32[16,1024]{1,0:T(8,128)S(1)} %get-tuple-element.194.leave_ref, bf16[1024,2048]{1,0:T(8,128)(2,1)S(1)} %get-tuple-element.112.k_ref, bf16[1024,2048]{1,0:T(8,128)(2,1)S(1)} %get-tuple-element.113.v_ref, ...), custom_call_target="tpu_custom_call" | custom-call | flops 1073741824 | bytes 8388608 | tf_op jit(solution)/shard_map/pallas_call | solution.py:302
  (30 shorter events, 3.2 us)
Async XLA Ops:
  6.9 7.9 %collective-permute-start = (f32[16,128,128]{2,1,0:T(8,128)S(1)}, f32[16,128,128]{2,1,0:T(8,128)S(1)}, u32[]{:S(2)}, u32[]{:S(2)}) collective-permute-start(f32[16,128,128]{2,1,0:T(8,128)S(1)} %get-tuple-element.106.state_ref), channel_id=1, source_target_pairs={{0,4},{4,0},{8,12},{12,8},{16,20},{20,16},{24,28},{28,24},{1,5},{5... | collective-permute-start | bytes 3145736 | tf_op jit(solution)/shard_map/ppermute | solution.py:322
  7.4 7.4 %collective-permute-start.1 = (f32[16,128]{1,0:T(8,128)S(1)}, f32[16,128]{1,0:T(8,128)S(1)}, u32[]{:S(2)}, u32[]{:S(2)}) collective-permute-start(f32[16,128]{1,0:T(8,128)S(1)} %get-tuple-element.109.pass_ref), channel_id=1, source_target_pairs={{0,4},{4,0},{8,12},{12,8},{16,20},{20,16},{24,28},{28,24},{1,5},{5... | collective-permute-start | bytes 24584 | tf_op jit(solution)/shard_map/ppermute | solution.py:322
  15.0 13.4 %collective-permute-start.2 = (f32[4,128,128]{2,1,0:T(8,128)S(1)}, f32[4,128,128]{2,1,0:T(8,128)S(1)}, u32[]{:S(2)}, u32[]{:S(2)}) collective-permute-start(f32[4,128,128]{2,1,0:T(8,128)S(1)} %get-tuple-element.117.to_x_ref), channel_id=1, source_target_pairs={{0,8},{4,12},{8,0},{12,4},{16,24},{20,28},{24,16},{28,20},{1,9},{5... | collective-permute-start | bytes 786440 | tf_op jit(solution)/shard_map/ppermute | solution.py:322
  17.9 10.5 %collective-permute-start.3 = (f32[4,128,128]{2,1,0:T(8,128)S(1)}, f32[4,128,128]{2,1,0:T(8,128)S(1)}, u32[]{:S(2)}, u32[]{:S(2)}) collective-permute-start(f32[4,128,128]{2,1,0:T(8,128)S(1)} %get-tuple-element.118.to_y_ref), channel_id=1, source_target_pairs={{0,16},{4,20},{8,24},{12,28},{16,0},{20,4},{24,8},{28,12},{1,17},{... | collective-permute-start | bytes 786440 | tf_op jit(solution)/shard_map/ppermute | solution.py:322
  19.5 8.9 %collective-permute-start.5 = (f32[16,128]{1,0:T(8,128)S(1)}, f32[16,128]{1,0:T(8,128)S(1)}, u32[]{:S(2)}, u32[]{:S(2)}) collective-permute-start(f32[16,128]{1,0:T(8,128)S(1)} %get-tuple-element.119.chip_ref), channel_id=1, source_target_pairs={{0,24},{4,28},{8,16},{12,20},{16,8},{20,12},{24,0},{28,4},{1,25},{... | collective-permute-start | bytes 24584 | tf_op jit(solution)/shard_map/ppermute | solution.py:322
  19.5 8.9 %collective-permute-start.4 = (f32[16,128]{1,0:T(8,128)S(1)}, f32[16,128]{1,0:T(8,128)S(1)}, u32[]{:S(2)}, u32[]{:S(2)}) collective-permute-start(f32[16,128]{1,0:T(8,128)S(1)} %get-tuple-element.119.chip_ref), channel_id=1, source_target_pairs={{0,8},{4,12},{8,0},{12,4},{16,24},{20,28},{24,16},{28,20},{1,9},{5... | collective-permute-start | bytes 24584 | tf_op jit(solution)/shard_map/ppermute | solution.py:322
  28.6 9.0 %collective-permute-start.6 = (f32[4,128,128]{2,1,0:T(8,128)S(1)}, f32[4,128,128]{2,1,0:T(8,128)S(1)}, u32[]{:S(2)}, u32[]{:S(2)}) collective-permute-start(f32[4,128,128]{2,1,0:T(8,128)S(1)} %get-tuple-element.130), channel_id=1, source_target_pairs={{0,16},{4,20},{8,24},{12,28},{16,0},{20,4},{24,8},{28,12},{1,17},{... | collective-permute-start | bytes 786440 | tf_op jit(solution)/shard_map/ppermute | solution.py:322
  30.2 7.4 %collective-permute-start.7 = (f32[4,128,128]{2,1,0:T(8,128)S(1)}, f32[4,128,128]{2,1,0:T(8,128)S(1)}, u32[]{:S(2)}, u32[]{:S(2)}) collective-permute-start(f32[4,128,128]{2,1,0:T(8,128)S(1)} %get-tuple-element.131), channel_id=1, source_target_pairs={{0,8},{4,12},{8,0},{12,4},{16,24},{20,28},{24,16},{28,20},{1,9},{5... | collective-permute-start | bytes 786440 | tf_op jit(solution)/shard_map/ppermute | solution.py:322
  37.7 7.0 %collective-permute-start.8 = (f32[8,128,128]{2,1,0:T(8,128)S(1)}, f32[8,128,128]{2,1,0:T(8,128)S(1)}, u32[]{:S(2)}, u32[]{:S(2)}) collective-permute-start(f32[8,128,128]{2,1,0:T(8,128)S(1)} %shard_map.126.refs_0_), channel_id=1, source_target_pairs={{0,4},{4,0},{8,12},{12,8},{16,20},{20,16},{24,28},{28,24},{1,5},{5... | collective-permute-start | bytes 1572872 | tf_op jit(solution)/shard_map/ppermute | solution.py:322
  52.5 3.7 %collective-permute-start.9 = (f32[2,1024]{1,0:T(2,128)S(1)}, f32[2,1024]{1,0:T(2,128)S(1)}, u32[]{:S(2)}, u32[]{:S(2)}) collective-permute-start(f32[2,1024]{1,0:T(2,128)S(1)} %get-tuple-element.151.a_ref), channel_id=1, source_target_pairs={{0,1},{1,0},{2,3},{3,2},{4,5},{5,4},{6,7},{7,6},{8,9},{9,8},{10,11... | collective-permute-start | bytes 24584 | tf_op jit(solution)/shard_map/ppermute | solution.py:593
  56.3 4.5 %collective-permute-start.10 = (f32[2,1024]{1,0:T(2,128)S(1)}, f32[2,1024]{1,0:T(2,128)S(1)}, u32[]{:S(2)}, u32[]{:S(2)}) collective-permute-start(f32[2,1024]{1,0:T(2,128)S(1)} %shard_map.129.refs_0_), channel_id=1, source_target_pairs={{0,2},{1,3},{2,0},{3,1},{4,6},{5,7},{6,4},{7,5},{8,10},{9,11},{10,... | collective-permute-start | bytes 24584 | tf_op jit(solution)/shard_map/ppermute | solution.py:596
  66.5 7.2 %collective-permute-start.11 = (f32[16,128,128]{2,1,0:T(8,128)S(1)}, f32[16,128,128]{2,1,0:T(8,128)S(1)}, u32[]{:S(2)}, u32[]{:S(2)}) collective-permute-start(f32[16,128,128]{2,1,0:T(8,128)S(1)} %get-tuple-element.154.state_ref), channel_id=1, source_target_pairs={{0,4},{4,0},{8,12},{12,8},{16,20},{20,16},{24,28},{28,24},{1,5},{5... | collective-permute-start | bytes 3145736 | tf_op jit(solution)/shard_map/ppermute | solution.py:322
  73.8 9.3 %collective-permute-start.12 = (f32[4,128,128]{2,1,0:T(8,128)S(1)}, f32[4,128,128]{2,1,0:T(8,128)S(1)}, u32[]{:S(2)}, u32[]{:S(2)}) collective-permute-start(f32[4,128,128]{2,1,0:T(8,128)S(1)} %get-tuple-element.163.to_x_ref), channel_id=1, source_target_pairs={{0,8},{4,12},{8,0},{12,4},{16,24},{20,28},{24,16},{28,20},{1,9},{5... | collective-permute-start | bytes 786440 | tf_op jit(solution)/shard_map/ppermute | solution.py:322
  75.4 8.5 %collective-permute-start.13 = (f32[4,128,128]{2,1,0:T(8,128)S(1)}, f32[4,128,128]{2,1,0:T(8,128)S(1)}, u32[]{:S(2)}, u32[]{:S(2)}) collective-permute-start(f32[4,128,128]{2,1,0:T(8,128)S(1)} %get-tuple-element.164.to_y_ref), channel_id=1, source_target_pairs={{0,16},{4,20},{8,24},{12,28},{16,0},{20,4},{24,8},{28,12},{1,17},{... | collective-permute-start | bytes 786440 | tf_op jit(solution)/shard_map/ppermute | solution.py:322
  84.1 8.6 %collective-permute-start.14 = (f32[4,128,128]{2,1,0:T(8,128)S(1)}, f32[4,128,128]{2,1,0:T(8,128)S(1)}, u32[]{:S(2)}, u32[]{:S(2)}) collective-permute-start(f32[4,128,128]{2,1,0:T(8,128)S(1)} %get-tuple-element.176), channel_id=1, source_target_pairs={{0,16},{4,20},{8,24},{12,28},{16,0},{20,4},{24,8},{28,12},{1,17},{... | collective-permute-start | bytes 786440 | tf_op jit(solution)/shard_map/ppermute | solution.py:322
  85.0 7.9 %collective-permute-start.15 = (f32[4,128,128]{2,1,0:T(8,128)S(1)}, f32[4,128,128]{2,1,0:T(8,128)S(1)}, u32[]{:S(2)}, u32[]{:S(2)}) collective-permute-start(f32[4,128,128]{2,1,0:T(8,128)S(1)} %get-tuple-element.177), channel_id=1, source_target_pairs={{0,8},{4,12},{8,0},{12,4},{16,24},{20,28},{24,16},{28,20},{1,9},{5... | collective-permute-start | bytes 786440 | tf_op jit(solution)/shard_map/ppermute | solution.py:322
  93.0 7.3 %collective-permute-start.16 = (f32[8,128,128]{2,1,0:T(8,128)S(1)}, f32[8,128,128]{2,1,0:T(8,128)S(1)}, u32[]{:S(2)}, u32[]{:S(2)}) collective-permute-start(f32[8,128,128]{2,1,0:T(8,128)S(1)} %shard_map.136.refs_0_), channel_id=1, source_target_pairs={{0,4},{4,0},{8,12},{12,8},{16,20},{20,16},{24,28},{28,24},{1,5},{5... | collective-permute-start | bytes 1572872 | tf_op jit(solution)/shard_map/ppermute | solution.py:322
where the time goes:
time: 109 us; the launch traced here: 108 us
  Pallas kernels  85.2 us (78%)
  starting transfers between devices  17.1 us (16%)
  waiting for transfers between devices  4.97 us (5%)
    pallas_call x20, Pallas kernels, call(): pl.pallas_call(kernel, grid=grid, in_specs=[spec for _, spec in ins], out...  85.2 us
    ppermute x15, starting transfers between devices, across(): return lax.ppermute(x, 'seq', [(i, i ^ flips) for i in range(devices)])  12.8 us
    ppermute x2, starting transfers between devices, body(): lax.ppermute(sums, 'head', [(i, i ^ apart) for i in range(parts)])  4.23 us
    ppermute x2, waiting for transfers between devices, body(): lax.ppermute(sums, 'head', [(i, i ^ apart) for i in range(parts)])  4.04 us
  transfers between devices with their start and end apart: 17, of which 4 were waited for; matrix products, arithmetic and copies ran while one was open for 0% of the time, Pallas kernels for 53%

commit v1 on v0

--- a/solution.py
+++ b/solution.py
@@ -42,6 +42,11 @@
 
 def head_span(head, count=1):
     return pl.ds(pl.multiple_of(head * HD, HD), count * HD)
+
+
+def save(stores):
+    for ref, index, value in stores:
+        ref[index] = value
 
 
 def sigmoid(x):
@@ -89,6 +94,7 @@
 
     for copy in copies(step):
         copy.wait()
+    late = []
     for g in range(GROUP):
         h = step * GROUP + g
         mine = head_span(h)
@@ -97,12 +103,14 @@
         for n, span in enumerate(spans(chunks)):
             keyed = (k_ref[span, mine].T.astype(F32) * leave_ref[pl.ds(h, 1), span]).astype(BF16)
             local = dot(keyed, v_ref[span, mine])
-            loc_ref[h, n] = local
             passing = enter_ref[pl.ds(h, 1), span][:, CHUNK - 1 : CHUNK]
             state = local if state is None else passing * state + local
             total = passing if total is None else passing * total
-        state_ref[h] = state
-        pass_ref[pl.ds(h, 1), :] = jnp.broadcast_to(total, (1, HD))
+            save(late)
+            late = [(loc_ref, (h, n), local)]
+        late.append((state_ref, h, state))
+        late.append((pass_ref, (pl.ds(h, 1), slice(None)), jnp.broadcast_to(total, (1, HD))))
+    save(late)
 
 
 def prepare_kernel(rrow_ref, crow_ref, enter_ref, mask_ref, cols_ref):
@@ -146,6 +154,7 @@
 
     cols_now = turned(cols_ref, first + step)
     copy(step).wait()
+    late = []
     for g in range(1):
         h = first + step
         cols = slice(g * HD, (g + 1) * HD)
@@ -155,12 +164,17 @@
             scores = dot(q, k_ref[span, mine], NT)
             c_row = crow_ref[pl.ds(h, 1), span]
             probs = decayed(scores, spread(cols_now[span], g), c_row, mask_ref.at[n])
-            probs_ref[g, n] = probs
-            attn_ref[span, mine] = dot(probs, v_ref[span, mine])
-            turned_q_ref[h, :, span] = q.T
+            inside = dot(probs, v_ref[span, mine])
             sig = sigmoid(gate_ref[span, cols].astype(F32))
             gnorm = grad_ref[span, cols].astype(F32) * sig * gain_ref[0:1, cols]
-            gnorm_ref[span, mine] = gnorm.astype(BF16)
+            save(late)
+            late = [
+                (probs_ref, (g, n), probs),
+                (attn_ref, (span, mine), inside),
+                (turned_q_ref, (h, slice(None), span), q.T),
+                (gnorm_ref, (span, mine), gnorm.astype(BF16)),
+            ]
+    save(late)
 
 
 def outside_kernel(chunks, entering, inputs, cols_ref, enter_ref, q_ref, gnorm_ref, loc_ref, *refs):
@@ -176,23 +190,24 @@
     heads = [step * GROUP + g for g in range(GROUP)]
     cols_now = turned(cols_ref, enter_ref.shape[0] + step * GROUP)
     carries = [entering(in_refs, h) for h in heads]
+    late = []
     for n, span in enumerate(spans(chunks)):
         squares = sq_ref[span, :]
         inners = inner_ref[span, :]
         for g, h in enumerate(heads):
             mine = head_span(h)
             held = carries[g].astype(BF16)
-            held_ref[h, n] = held
             enter = spread(cols_now[span], g)
             attn = inside_ref[span, mine] + enter * dot(q_ref[span, mine], held)
-            attn_ref[span, mine] = attn
             squares = squares + attn * attn
             inners = inners + gnorm_ref[span, mine].astype(F32) * attn
             if n + 1 < chunks:
                 passing = enter_ref[pl.ds(h, 1), span][:, CHUNK - 1 : CHUNK]
                 carries[g] = passing * carries[g] + loc_ref[h, n]
-        sq_ref[span, :] = squares
-        inner_ref[span, :] = inners
+            save(late)
+            late = [(held_ref, (h, n), held), (attn_ref, (span, mine), attn)]
+        late += [(sq_ref, (span, slice(None)), squares), (inner_ref, (span, slice(None)), inners)]
+    save(late)
 
     @pl.when(step == pl.num_programs(0) - 1)
     def _():
@@ -214,6 +229,7 @@
         alpha_ref[...] = column(inverse)
         beta_ref[...] = column(inverse * inverse * inverse * sums[1:2] / WIDTH)
 
+    late = []
     for g in range(GROUP):
         h = step * GROUP + g
         mine = head_span(h)
@@ -223,13 +239,17 @@
             gnorm = gnorm_ref[span, mine].astype(F32)
             agrad = alpha_ref[span, :] * gnorm - attn_ref[span, mine] * beta_ref[span, :]
             agrad = agrad.astype(BF16)
-            agrad_ref[span, mine] = agrad
-            turned_ref[h, :, span] = agrad.T
             qkeyed = (turned_q_ref[h, :, span].astype(F32) * enter).astype(BF16)
             local = dot(qkeyed, agrad)
-            bloc_ref[h, n] = local
             back = local if back is None else local + enter[:, CHUNK - 1 : CHUNK] * back
-        back_ref[h] = back
+            save(late)
+            late = [
+                (agrad_ref, (span, mine), agrad),
+                (turned_ref, (h, slice(None), span), agrad.T),
+                (bloc_ref, (h, n), local),
+            ]
+        late.append((back_ref, h, back))
+    save(late)
 
 
 def inner_grad_kernel(
@@ -239,6 +259,7 @@
     dk_ref, dv_ref, dq_ref, gated_ref, ggate_ref = refs[-5:]
     step = pl.program_id(0)
     cols_now = turned(cols_ref, first + step)
+    late = []
     for g in range(1):
         h = first + step
         cols = slice(g * HD, (g + 1) * HD)
@@ -249,21 +270,29 @@
             c_row = crow_ref[pl.ds(h, 1), span]
             dscore = decayed(both[:, :CHUNK], spread(cols_now[span], g), c_row, mask_ref.at[n])
             enter = spread(cols_now[span], crow_ref.shape[0] + g)
-            dq_ref[span, cols] = (dot(dscore, k) + enter * both[:, CHUNK:]).astype(BF16)
-            dv_ref[h, :, span] = dot(turned_agrad_ref[h, :, span], probs_ref[g, n]).astype(BF16)
-            dk_ref[h, :, span] = dot(turned_q_ref[h, :, span], dscore).astype(BF16)
+            dq = dot(dscore, k) + enter * both[:, CHUNK:]
+            dv = dot(turned_agrad_ref[h, :, span], probs_ref[g, n])
+            dk = dot(turned_q_ref[h, :, span], dscore)
             normed = attn_ref[span, mine] * alpha_ref[span, :] * gain_ref[0:1, cols]
             sig = sigmoid(gate_ref[span, cols].astype(F32))
             gated = normed * sig
-            gated_ref[span, cols] = gated.astype(BF16)
             ggate = grad_ref[span, cols].astype(F32) * gated * (1.0 - sig)
-            ggate_ref[span, cols] = ggate.astype(BF16)
+            save(late)
+            late = [
+                (dq_ref, (span, cols), dq.astype(BF16)),
+                (dv_ref, (h, slice(None), span), dv.astype(BF16)),
+                (dk_ref, (h, slice(None), span), dk.astype(BF16)),
+                (gated_ref, (span, cols), gated.astype(BF16)),
+                (ggate_ref, (span, cols), ggate.astype(BF16)),
+            ]
+    save(late)
 
 
 def outer_grad_kernel(chunks, entering, inputs, enter_ref, leave_ref, k_ref, v_ref, *refs):
     in_refs = refs[:inputs]
     dkin_ref, dvin_ref, bloc_ref, dk_ref, dv_ref = refs[inputs:]
     step = pl.program_id(0)
+    late = []
     for g in range(GROUP):
         h = step * GROUP + g
         cols = slice(g * HD, (g + 1) * HD)
@@ -274,11 +303,15 @@
             back = carry.astype(BF16)
             dk = dkin_ref[h, :, span].astype(F32) + leave * dot(back, v_ref[span, mine], NT)
             dv = dvin_ref[h, :, span].astype(F32) + leave * dot(back.T, k_ref[span, mine], NT)
-            dk_ref[span, cols] = dk.astype(BF16).T
-            dv_ref[span, cols] = dv.astype(BF16).T
             if n > 0:
                 passing = enter_ref[pl.ds(h, 1), span][:, CHUNK - 1 : CHUNK]
                 carry = bloc_ref[h, n] + passing * carry
+            save(late)
+            late = [
+                (dk_ref, (span, cols), dk.astype(BF16).T),
+                (dv_ref, (span, cols), dv.astype(BF16).T),
+            ]
+    save(late)
 
 
 def hbm(x):

time: 109 us -> 110 us (level)
  transfers between devices with their start and end apart: 17 -> 17, of which waited for: 4 -> 3; matrix products, arithmetic and copies ran while one was open for 0% -> 0% of each run, Pallas kernels for 53% -> 53%
where the time goes in v1:
time: 110 us; the launch traced here: 109 us
  Pallas kernels  86 us (78%)
  starting transfers between devices  17.2 us (16%)
  waiting for transfers between devices  4.69 us (4%)
    pallas_call x20, Pallas kernels, call(): pl.pallas_call(kernel, grid=grid, in_specs=[spec for _, spec in ins], out...  86 us
    ppermute x15, starting transfers between devices, across(): return lax.ppermute(x, 'seq', [(i, i ^ flips) for i in range(devices)])  13 us
    ppermute x2, starting transfers between devices, body(): lax.ppermute(sums, 'head', [(i, i ^ apart) for i in range(parts)])  4.23 us
    ppermute x2, waiting for transfers between devices, body(): lax.ppermute(sums, 'head', [(i, i ^ apart) for i in range(parts)])  4.04 us
  transfers between devices with their start and end apart: 17, of which 3 were waited for; matrix products, arithmetic and copies ran while one was open for 0% of the time, Pallas kernels for 53%

profile of v1, /device:TPU:0, one launch (start us, length us, event | category | flops | bytes accessed | tf_op | source)
XLA Modules:
  0.0 108.7 jit_solution(4881268770801683366)
XLA Ops:
  0.6 6.3 %shard_map.119 = (f32[16,1024]{1,0:T(8,128)S(1)}, f32[16,1024]{1,0:T(8,128)S(1)}, f32[16,1024]{1,0:T(8,128)S(1)}, f32[8,1024]{1,0:T(8,128)S(1)}, bf16[1024,2048]...) custom-call(f32[16,1024]{1,0:T(8,128)} %lc_ref.1, ...), custom_call_target="tpu_custom_call" | custom-call | flops 536870912 | bytes 8388608 | tf_op jit(solution)/shard_map/pallas_call | solution.py:335
  6.9 0.5 collective-permute-start
  7.8 7.0 %shard_map.121 = (f32[1024,2048]{1,0:T(8,128)S(1)}, bf16[1024,2048]{1,0:T(8,128)(2,1)S(1)}, bf16[1024,2048]{1,0:T(8,128)(2,1)S(1)}, bf16[16,128,1024]{2,1,0:T(8,128)(2,1)S(1)}, bf16[4,4,256,256]{3,2,1,0:T(8,128)(2,1)}) custom-call(f32[16,1024]{1,0:T(8,128)S(1)} %get-tuple-element.186.crow_ref, f32[1024,128]{1,0:T(8,128)S(1)} %get-tuple-element.108.cols_ref, ...), custom_call_target="tpu_custom_call" | custom-call | flops 536870912 | bytes 5242880 | tf_op jit(solution)/shard_map/pallas_call | solution.py:335
  15.0 3.0 %collective-permute-start.2 = (f32[4,128,128]{2,1,0:T(8,128)S(1)}, f32[4,128,128]{2,1,0:T(8,128)S(1)}, u32[]{:S(2)}, u32[]{:S(2)}) collective-permute-start(f32[4,128,128]{2,1,0:T(8,128)S(1)} %get-tuple-element.117.to_x_ref), channel_id=1, source_target_pairs={{0,8},{4,12},{8,0},{12,4},{16,24},{20,28},{24,16},{28,20},{1,9},{5... | collective-permute-start | bytes 786440 | tf_op jit(solution)/shard_map/ppermute | solution.py:355
  18.0 1.5 %collective-permute-start.3 = (f32[4,128,128]{2,1,0:T(8,128)S(1)}, f32[4,128,128]{2,1,0:T(8,128)S(1)}, u32[]{:S(2)}, u32[]{:S(2)}) collective-permute-start(f32[4,128,128]{2,1,0:T(8,128)S(1)} %get-tuple-element.118.to_y_ref), channel_id=1, source_target_pairs={{0,16},{4,20},{8,24},{12,28},{16,0},{20,4},{24,8},{28,12},{1,17},{... | collective-permute-start | bytes 786440 | tf_op jit(solution)/shard_map/ppermute | solution.py:355
  19.5 1.9 %collective-permute-start.4 = (f32[16,128]{1,0:T(8,128)S(1)}, f32[16,128]{1,0:T(8,128)S(1)}, u32[]{:S(2)}, u32[]{:S(2)}) collective-permute-start(f32[16,128]{1,0:T(8,128)S(1)} %get-tuple-element.119.chip_ref), channel_id=1, source_target_pairs={{0,8},{4,12},{8,0},{12,4},{16,24},{20,28},{24,16},{28,20},{1,9},{5... | collective-permute-start | bytes 24584 | tf_op jit(solution)/shard_map/ppermute | solution.py:355
  21.5 7.0 %shard_map.123 = (f32[1024,2048]{1,0:T(8,128)S(1)}, bf16[1024,2048]{1,0:T(8,128)(2,1)S(1)}, bf16[1024,2048]{1,0:T(8,128)(2,1)S(1)}, bf16[16,128,1024]{2,1,0:T(8,128)(2,1)S(1)}, bf16[4,4,256,256]{3,2,1,0:T(8,128)(2,1)}) custom-call(f32[16,1024]{1,0:T(8,128)S(1)} %get-tuple-element.186.crow_, ...), custom_call_target="tpu_custom_call", output_to_operand_aliasing={{0}: (9, {}), {1}: (10, {}), {2}: (11, {}), {3}: (12, {})} | custom-call | flops 536870912 | bytes 5242880 | tf_op jit(solution)/shard_map/pallas_call | solution.py:335
  28.7 1.6 %collective-permute-start.6 = (f32[4,128,128]{2,1,0:T(8,128)S(1)}, f32[4,128,128]{2,1,0:T(8,128)S(1)}, u32[]{:S(2)}, u32[]{:S(2)}) collective-permute-start(f32[4,128,128]{2,1,0:T(8,128)S(1)} %get-tuple-element.130), channel_id=1, source_target_pairs={{0,16},{4,20},{8,24},{12,28},{16,0},{20,4},{24,8},{28,12},{1,17},{... | collective-permute-start | bytes 786440 | tf_op jit(solution)/shard_map/ppermute | solution.py:355
  30.8 7.0 %shard_map.125 = (f32[1024,2048]{1,0:T(8,128)S(1)}, bf16[1024,2048]{1,0:T(8,128)(2,1)S(1)}, bf16[1024,2048]{1,0:T(8,128)(2,1)S(1)}, bf16[16,128,1024]{2,1,0:T(8,128)(2,1)S(1)}, bf16[4,4,256,256]{3,2,1,0:T(8,128)(2,1)}) custom-call(f32[16,1024]{1,0:T(8,128)S(1)} %get-tuple-element.186.crow_, ...), custom_call_target="tpu_custom_call", output_to_operand_aliasing={{0}: (9, {}), {1}: (10, {}), {2}: (11, {}), {3}: (12, {})} | custom-call | flops 536870912 | bytes 5242880 | tf_op jit(solution)/shard_map/pallas_call | solution.py:335
  38.0 7.0 %shard_map.127 = (f32[1024,2048]{1,0:T(8,128)S(1)}, bf16[1024,2048]{1,0:T(8,128)(2,1)S(1)}, bf16[1024,2048]{1,0:T(8,128)(2,1)S(1)}, bf16[16,128,1024]{2,1,0:T(8,128)(2,1)S(1)}, bf16[4,4,256,256]{3,2,1,0:T(8,128)(2,1)}) custom-call(f32[16,1024]{1,0:T(8,128)S(1)} %get-tuple-element.186.crow_, ...), custom_call_target="tpu_custom_call", output_to_operand_aliasing={{0}: (9, {}), {1}: (10, {}), {2}: (11, {}), {3}: (12, {})} | custom-call | flops 536870912 | bytes 5242880 | tf_op jit(solution)/shard_map/pallas_call | solution.py:335
  45.0 7.7 %shard_map.128 = (f32[1024,2048]{1,0:T(8,128)S(1)}, bf16[16,4,128,128]{3,2,1,0:T(8,128)(2,1)S(1)}, f32[2,1024]{1,0:T(2,128)S(1)}) custom-call(f32[1024,128]{1,0:T(8,128)S(1)} %get-tuple-element.108.cols_ref, f32[16,1024]{1,0:T(8,128)S(1)} %get-tuple-element.104.enter_ref, ...), custom_call_target="tpu_custom_call", output_to_operand_aliasing={{0}: (9, {})} | custom-call | flops 536870912 | bytes 4194304 | tf_op jit(solution)/shard_map/pallas_call | solution.py:335
  52.7 1.6 %collective-permute-start.9 = (f32[2,1024]{1,0:T(2,128)S(1)}, f32[2,1024]{1,0:T(2,128)S(1)}, u32[]{:S(2)}, u32[]{:S(2)}) collective-permute-start(f32[2,1024]{1,0:T(2,128)S(1)} %get-tuple-element.151.a_ref), channel_id=1, source_target_pairs={{0,1},{1,0},{2,3},{3,2},{4,5},{5,4},{6,7},{7,6},{8,9},{9,8},{10,11... | collective-permute-start | bytes 24584 | tf_op jit(solution)/shard_map/ppermute | solution.py:626
  54.4 2.1 %collective-permute-done.9.b_ref = f32[2,1024]{1,0:T(2,128)S(1)} collective-permute-done((f32[2,1024]{1,0:T(2,128)S(1)}, f32[2,1024]{1,0:T(2,128)S(1)}, u32[]{:S(2)}, u32[]{:S(2)}) %collective-permute-start.9) | collective-permute-done | bytes 8224 | tf_op jit(solution)/shard_map/ppermute | solution.py:626
  56.5 2.6 %collective-permute-start.10 = (f32[2,1024]{1,0:T(2,128)S(1)}, f32[2,1024]{1,0:T(2,128)S(1)}, u32[]{:S(2)}, u32[]{:S(2)}) collective-permute-start(f32[2,1024]{1,0:T(2,128)S(1)} %shard_map.129.refs_0_), channel_id=1, source_target_pairs={{0,2},{1,3},{2,0},{3,1},{4,6},{5,7},{6,4},{7,5},{8,10},{9,11},{10,... | collective-permute-start | bytes 24584 | tf_op jit(solution)/shard_map/ppermute | solution.py:629
  59.0 2.0 %collective-permute-done.10.refs_1_ = f32[2,1024]{1,0:T(2,128)S(1)} collective-permute-done((f32[2,1024]{1,0:T(2,128)S(1)}, f32[2,1024]{1,0:T(2,128)S(1)}, u32[]{:S(2)}, u32[]{:S(2)}) %collective-permute-start.10) | collective-permute-done | bytes 8224 | tf_op jit(solution)/shard_map/ppermute | solution.py:629
  61.0 5.6 %shard_map.130 = (bf16[1024,2048]{1,0:T(8,128)(2,1)S(1)}, bf16[16,128,1024]{2,1,0:T(8,128)(2,1)S(1)}, f32[16,4,128,128]{3,2,1,0:T(8,128)S(1)}, f32[16,128,128]{2...) custom-call(f32[16,1024]{1,0:T(8,128)S(1)} %get-tuple-element.104.enter_ref, ...), custom_call_target="tpu_custom_call" | custom-call | flops 536870912 | bytes 4194304 | tf_op jit(solution)/shard_map/pallas_call | solution.py:335
  66.6 7.3 %shard_map.131 = (bf16[16,128,1024]{2,1,0:T(8,128)(2,1)S(1)}, bf16[16,128,1024]{2,1,0:T(8,128)(2,1)S(1)}, bf16[1024,2048]{1,0:T(8,128)(2,1)}, bf16[1024,2048]{1,0:T(8,128)(2,1)}, bf16[1024,2048]{1,0:T(8,128)(2,1)}) custom-call(f32[16,1024]{1,0:T(8,128)S(1)} %get-tuple-element.186.crow_ref, ...), custom_call_target="tpu_custom_call", output_to_operand_aliasing={{0}: (9, {}), {1}: (10, {})} | custom-call | flops 1207959552 | bytes 7340032 | tf_op jit(solution)/shard_map/pallas_call | solution.py:335
  74.1 1.6 %collective-permute-start.12 = (f32[4,128,128]{2,1,0:T(8,128)S(1)}, f32[4,128,128]{2,1,0:T(8,128)S(1)}, u32[]{:S(2)}, u32[]{:S(2)}) collective-permute-start(f32[4,128,128]{2,1,0:T(8,128)S(1)} %get-tuple-element.163.to_x_ref), channel_id=1, source_target_pairs={{0,8},{4,12},{8,0},{12,4},{16,24},{20,28},{24,16},{28,20},{1,9},{5... | collective-permute-start | bytes 786440 | tf_op jit(solution)/shard_map/ppermute | solution.py:355
  76.2 7.4 %shard_map.133 = (bf16[16,128,1024]{2,1,0:T(8,128)(2,1)S(1)}, bf16[16,128,1024]{2,1,0:T(8,128)(2,1)S(1)}, bf16[1024,2048]{1,0:T(8,128)(2,1)}, bf16[1024,2048]{1,0:T(8,128)(2,1)}, bf16[1024,2048]{1,0:T(8,128)(2,1)}) custom-call(f32[16,1024]{1,0:T(8,128)S(1)} %get-tuple-element.186.crow_, ...), custom_call_target="tpu_custom_call", output_to_operand_aliasing={{0}: (9, {}), {1}: (10, {}), {2}: (15, {}), {3}: (16, {}), ... | custom-call | flops 1207959552 | bytes 7340032 | tf_op jit(solution)/shard_map/pallas_call | solution.py:335
  83.5 0.6 collective-permute-done.13.from_y_ref
  84.4 1.0 collective-permute-start.14
  86.0 7.3 %shard_map.135 = (bf16[16,128,1024]{2,1,0:T(8,128)(2,1)S(1)}, bf16[16,128,1024]{2,1,0:T(8,128)(2,1)S(1)}, bf16[1024,2048]{1,0:T(8,128)(2,1)}, bf16[1024,2048]{1,0:T(8,128)(2,1)}, bf16[1024,2048]{1,0:T(8,128)(2,1)}) custom-call(f32[16,1024]{1,0:T(8,128)S(1)} %get-tuple-element.186.crow_, ...), custom_call_target="tpu_custom_call", output_to_operand_aliasing={{0}: (9, {}), {1}: (10, {}), {2}: (15, {}), {3}: (16, {}), ... | custom-call | flops 1207959552 | bytes 7340032 | tf_op jit(solution)/shard_map/pallas_call | solution.py:335
  93.5 7.4 %shard_map.137 = (bf16[16,128,1024]{2,1,0:T(8,128)(2,1)S(1)}, bf16[16,128,1024]{2,1,0:T(8,128)(2,1)S(1)}, bf16[1024,2048]{1,0:T(8,128)(2,1)}, bf16[1024,2048]{1,0:T(8,128)(2,1)}, bf16[1024,2048]{1,0:T(8,128)(2,1)}) custom-call(f32[16,1024]{1,0:T(8,128)S(1)} %get-tuple-element.186.crow_, ...), custom_call_target="tpu_custom_call", output_to_operand_aliasing={{0}: (9, {}), {1}: (10, {}), {2}: (15, {}), {3}: (16, {}), ... | custom-call | flops 1207959552 | bytes 7340032 | tf_op jit(solution)/shard_map/pallas_call | solution.py:335
  100.9 7.7 %shard_map.138 = (bf16[1024,2048]{1,0:T(8,128)(2,1)}, bf16[1024,2048]{1,0:T(8,128)(2,1)}) custom-call(f32[16,1024]{1,0:T(8,128)S(1)} %get-tuple-element.104.enter_ref, f32[16,1024]{1,0:T(8,128)S(1)} %get-tuple-element.194.leave_ref, bf16[1024,2048]{1,0:T(8,128)(2,1)S(1)} %get-tuple-element.112.k_ref, bf16[1024,2048]{1,0:T(8,128)(2,1)S(1)} %get-tuple-element.113.v_ref, ...), custom_call_target="tpu_custom_call" | custom-call | flops 1073741824 | bytes 8388608 | tf_op jit(solution)/shard_map/pallas_call | solution.py:335
  (30 shorter events, 3.1 us)
Async XLA Ops:
  6.9 7.9 %collective-permute-start = (f32[16,128,128]{2,1,0:T(8,128)S(1)}, f32[16,128,128]{2,1,0:T(8,128)S(1)}, u32[]{:S(2)}, u32[]{:S(2)}) collective-permute-start(f32[16,128,128]{2,1,0:T(8,128)S(1)} %get-tuple-element.106.state_ref), channel_id=1, source_target_pairs={{0,4},{4,0},{8,12},{12,8},{16,20},{20,16},{24,28},{28,24},{1,5},{5... | collective-permute-start | bytes 3145736 | tf_op jit(solution)/shard_map/ppermute | solution.py:355
  7.4 7.4 %collective-permute-start.1 = (f32[16,128]{1,0:T(8,128)S(1)}, f32[16,128]{1,0:T(8,128)S(1)}, u32[]{:S(2)}, u32[]{:S(2)}) collective-permute-start(f32[16,128]{1,0:T(8,128)S(1)} %get-tuple-element.109.pass_ref), channel_id=1, source_target_pairs={{0,4},{4,0},{8,12},{12,8},{16,20},{20,16},{24,28},{28,24},{1,5},{5... | collective-permute-start | bytes 24584 | tf_op jit(solution)/shard_map/ppermute | solution.py:355
  15.0 13.5 %collective-permute-start.2 = (f32[4,128,128]{2,1,0:T(8,128)S(1)}, f32[4,128,128]{2,1,0:T(8,128)S(1)}, u32[]{:S(2)}, u32[]{:S(2)}) collective-permute-start(f32[4,128,128]{2,1,0:T(8,128)S(1)} %get-tuple-element.117.to_x_ref), channel_id=1, source_target_pairs={{0,8},{4,12},{8,0},{12,4},{16,24},{20,28},{24,16},{28,20},{1,9},{5... | collective-permute-start | bytes 786440 | tf_op jit(solution)/shard_map/ppermute | solution.py:355
  18.0 10.5 %collective-permute-start.3 = (f32[4,128,128]{2,1,0:T(8,128)S(1)}, f32[4,128,128]{2,1,0:T(8,128)S(1)}, u32[]{:S(2)}, u32[]{:S(2)}) collective-permute-start(f32[4,128,128]{2,1,0:T(8,128)S(1)} %get-tuple-element.118.to_y_ref), channel_id=1, source_target_pairs={{0,16},{4,20},{8,24},{12,28},{16,0},{20,4},{24,8},{28,12},{1,17},{... | collective-permute-start | bytes 786440 | tf_op jit(solution)/shard_map/ppermute | solution.py:355
  19.5 9.0 %collective-permute-start.5 = (f32[16,128]{1,0:T(8,128)S(1)}, f32[16,128]{1,0:T(8,128)S(1)}, u32[]{:S(2)}, u32[]{:S(2)}) collective-permute-start(f32[16,128]{1,0:T(8,128)S(1)} %get-tuple-element.119.chip_ref), channel_id=1, source_target_pairs={{0,24},{4,28},{8,16},{12,20},{16,8},{20,12},{24,0},{28,4},{1,25},{... | collective-permute-start | bytes 24584 | tf_op jit(solution)/shard_map/ppermute | solution.py:355
  19.5 8.9 %collective-permute-start.4 = (f32[16,128]{1,0:T(8,128)S(1)}, f32[16,128]{1,0:T(8,128)S(1)}, u32[]{:S(2)}, u32[]{:S(2)}) collective-permute-start(f32[16,128]{1,0:T(8,128)S(1)} %get-tuple-element.119.chip_ref), channel_id=1, source_target_pairs={{0,8},{4,12},{8,0},{12,4},{16,24},{20,28},{24,16},{28,20},{1,9},{5... | collective-permute-start | bytes 24584 | tf_op jit(solution)/shard_map/ppermute | solution.py:355
  28.7 9.1 %collective-permute-start.6 = (f32[4,128,128]{2,1,0:T(8,128)S(1)}, f32[4,128,128]{2,1,0:T(8,128)S(1)}, u32[]{:S(2)}, u32[]{:S(2)}) collective-permute-start(f32[4,128,128]{2,1,0:T(8,128)S(1)} %get-tuple-element.130), channel_id=1, source_target_pairs={{0,16},{4,20},{8,24},{12,28},{16,0},{20,4},{24,8},{28,12},{1,17},{... | collective-permute-start | bytes 786440 | tf_op jit(solution)/shard_map/ppermute | solution.py:355
  30.3 7.5 %collective-permute-start.7 = (f32[4,128,128]{2,1,0:T(8,128)S(1)}, f32[4,128,128]{2,1,0:T(8,128)S(1)}, u32[]{:S(2)}, u32[]{:S(2)}) collective-permute-start(f32[4,128,128]{2,1,0:T(8,128)S(1)} %get-tuple-element.131), channel_id=1, source_target_pairs={{0,8},{4,12},{8,0},{12,4},{16,24},{20,28},{24,16},{28,20},{1,9},{5... | collective-permute-start | bytes 786440 | tf_op jit(solution)/shard_map/ppermute | solution.py:355
  37.9 7.1 %collective-permute-start.8 = (f32[8,128,128]{2,1,0:T(8,128)S(1)}, f32[8,128,128]{2,1,0:T(8,128)S(1)}, u32[]{:S(2)}, u32[]{:S(2)}) collective-permute-start(f32[8,128,128]{2,1,0:T(8,128)S(1)} %shard_map.126.refs_0_), channel_id=1, source_target_pairs={{0,4},{4,0},{8,12},{12,8},{16,20},{20,16},{24,28},{28,24},{1,5},{5... | collective-permute-start | bytes 1572872 | tf_op jit(solution)/shard_map/ppermute | solution.py:355
  52.7 3.7 %collective-permute-start.9 = (f32[2,1024]{1,0:T(2,128)S(1)}, f32[2,1024]{1,0:T(2,128)S(1)}, u32[]{:S(2)}, u32[]{:S(2)}) collective-permute-start(f32[2,1024]{1,0:T(2,128)S(1)} %get-tuple-element.151.a_ref), channel_id=1, source_target_pairs={{0,1},{1,0},{2,3},{3,2},{4,5},{5,4},{6,7},{7,6},{8,9},{9,8},{10,11... | collective-permute-start | bytes 24584 | tf_op jit(solution)/shard_map/ppermute | solution.py:626
  56.5 4.5 %collective-permute-start.10 = (f32[2,1024]{1,0:T(2,128)S(1)}, f32[2,1024]{1,0:T(2,128)S(1)}, u32[]{:S(2)}, u32[]{:S(2)}) collective-permute-start(f32[2,1024]{1,0:T(2,128)S(1)} %shard_map.129.refs_0_), channel_id=1, source_target_pairs={{0,2},{1,3},{2,0},{3,1},{4,6},{5,7},{6,4},{7,5},{8,10},{9,11},{10,... | collective-permute-start | bytes 24584 | tf_op jit(solution)/shard_map/ppermute | solution.py:629
  66.6 7.3 %collective-permute-start.11 = (f32[16,128,128]{2,1,0:T(8,128)S(1)}, f32[16,128,128]{2,1,0:T(8,128)S(1)}, u32[]{:S(2)}, u32[]{:S(2)}) collective-permute-start(f32[16,128,128]{2,1,0:T(8,128)S(1)} %get-tuple-element.154.state_ref), channel_id=1, source_target_pairs={{0,4},{4,0},{8,12},{12,8},{16,20},{20,16},{24,28},{28,24},{1,5},{5... | collective-permute-start | bytes 3145736 | tf_op jit(solution)/shard_map/ppermute | solution.py:355
  74.1 9.5 %collective-permute-start.12 = (f32[4,128,128]{2,1,0:T(8,128)S(1)}, f32[4,128,128]{2,1,0:T(8,128)S(1)}, u32[]{:S(2)}, u32[]{:S(2)}) collective-permute-start(f32[4,128,128]{2,1,0:T(8,128)S(1)} %get-tuple-element.163.to_x_ref), channel_id=1, source_target_pairs={{0,8},{4,12},{8,0},{12,4},{16,24},{20,28},{24,16},{28,20},{1,9},{5... | collective-permute-start | bytes 786440 | tf_op jit(solution)/shard_map/ppermute | solution.py:355
  75.7 8.5 %collective-permute-start.13 = (f32[4,128,128]{2,1,0:T(8,128)S(1)}, f32[4,128,128]{2,1,0:T(8,128)S(1)}, u32[]{:S(2)}, u32[]{:S(2)}) collective-permute-start(f32[4,128,128]{2,1,0:T(8,128)S(1)} %get-tuple-element.164.to_y_ref), channel_id=1, source_target_pairs={{0,16},{4,20},{8,24},{12,28},{16,0},{20,4},{24,8},{28,12},{1,17},{... | collective-permute-start | bytes 786440 | tf_op jit(solution)/shard_map/ppermute | solution.py:355
  84.4 8.9 %collective-permute-start.14 = (f32[4,128,128]{2,1,0:T(8,128)S(1)}, f32[4,128,128]{2,1,0:T(8,128)S(1)}, u32[]{:S(2)}, u32[]{:S(2)}) collective-permute-start(f32[4,128,128]{2,1,0:T(8,128)S(1)} %get-tuple-element.176), channel_id=1, source_target_pairs={{0,16},{4,20},{8,24},{12,28},{16,0},{20,4},{24,8},{28,12},{1,17},{... | collective-permute-start | bytes 786440 | tf_op jit(solution)/shard_map/ppermute | solution.py:355
  85.4 7.9 %collective-permute-start.15 = (f32[4,128,128]{2,1,0:T(8,128)S(1)}, f32[4,128,128]{2,1,0:T(8,128)S(1)}, u32[]{:S(2)}, u32[]{:S(2)}) collective-permute-start(f32[4,128,128]{2,1,0:T(8,128)S(1)} %get-tuple-element.177), channel_id=1, source_target_pairs={{0,8},{4,12},{8,0},{12,4},{16,24},{20,28},{24,16},{28,20},{1,9},{5... | collective-permute-start | bytes 786440 | tf_op jit(solution)/shard_map/ppermute | solution.py:355
  93.4 7.5 %collective-permute-start.16 = (f32[8,128,128]{2,1,0:T(8,128)S(1)}, f32[8,128,128]{2,1,0:T(8,128)S(1)}, u32[]{:S(2)}, u32[]{:S(2)}) collective-permute-start(f32[8,128,128]{2,1,0:T(8,128)S(1)} %shard_map.136.refs_0_), channel_id=1, source_target_pairs={{0,4},{4,0},{8,12},{12,8},{16,20},{20,16},{24,28},{28,24},{1,5},{5... | collective-permute-start | bytes 1572872 | tf_op jit(solution)/shard_map/ppermute | solution.py:355

commit v2 on v1

--- a/solution.py
+++ b/solution.py
@@ -11,7 +11,9 @@
 HD = 128
 CHUNK = 256
 GROUP = 2
+RING = 1
 WINDOWS = 4
+ROOM = 4
 WIDTH = HEAD_TOTAL * HD
 
 epsilon = 1e-06
@@ -65,11 +67,62 @@
     return jnp.broadcast_to(row, (HD, row.shape[1])).T
 
 
+def start(copies):
+    for copy in copies:
+        copy.start()
+
+
+def wait(copies):
+    for copy in copies:
+        copy.wait()
+
+
+def group_of(at):
+    return head_span(at * RING, RING)
+
+
+def fetch_gates(at, gate_hbm, grad_hbm, gate_ring, grad_ring, sems):
+    slot = at % 2
+    return [
+        pltpu.make_async_copy(gate_hbm.at[:, group_of(at)], gate_ring.at[slot], sems.at[0]),
+        pltpu.make_async_copy(grad_hbm.at[:, group_of(at)], grad_ring.at[slot], sems.at[1]),
+    ]
+
+
+def fetch_q(at, q_hbm, q_ref, sem):
+    return [pltpu.make_async_copy(q_hbm.at[:, group_of(at)], q_ref.at[:, group_of(at)], sem)]
+
+
+def fetch_probs(at, probs_hbm, probs_ring, sem):
+    heads = pl.ds(at * RING, RING)
+    return [pltpu.make_async_copy(probs_hbm.at[heads], probs_ring.at[at % 2], sem)]
+
+
+def put_probs(at, probs_ring, probs_hbm, sem):
+    heads = pl.ds(at * RING, RING)
+    return [pltpu.make_async_copy(probs_ring.at[at % 2], probs_hbm.at[heads], sem)]
+
+
+def put_outs(at, out_ring, outs_hbm, sems):
+    return [
+        pltpu.make_async_copy(out_ring.at[at % 2, i], out.at[:, group_of(at)], sems.at[i])
+        for i, out in enumerate(outs_hbm)
+    ]
+
+
 def state_kernel(
-    chunks, steps, lc_ref, doc_ref, k_hbm, v_hbm,
-    crow_ref, enter_ref, leave_ref, rrow_ref, k_ref, v_ref, loc_ref, state_ref, pass_ref, sems,
+    chunks, steps, lc_hbm, doc_hbm, gain_hbm, k_hbm, v_hbm, q_hbm, gate_hbm, grad_hbm,
+    crow_ref, enter_ref, leave_ref, rrow_ref, k_ref, v_ref, loc_ref, state_ref, pass_ref,
+    gain_ref, q_ref, gate_ring, grad_ring, lc_ref, doc_ref, sems, small_sems, next_sems,
 ):
     step = pl.program_id(0)
+    small = [
+        pltpu.make_async_copy(lc_hbm, lc_ref, small_sems.at[0]),
+        pltpu.make_async_copy(doc_hbm, doc_ref, small_sems.at[1]),
+        pltpu.make_async_copy(gain_hbm, gain_ref, small_sems.at[2]),
+    ]
+    following = fetch_gates(0, gate_hbm, grad_hbm, gate_ring, grad_ring, next_sems)
+    following += fetch_q(0, q_hbm, q_ref, next_sems.at[2])
 
     def copies(at):
         here = head_span(at * GROUP, GROUP)
@@ -80,9 +133,11 @@
 
     @pl.when(step == 0)
     def _():
+        start(small)
         for at in range(steps):
-            for copy in copies(at):
-                copy.start()
+            start(copies(at))
+        start(following)
+        wait(small)
         c = chunk_cumsum(lc_ref[...] * LOG2E)
         r = chunk_cumsum(jnp.broadcast_to(doc_ref[...].astype(F32), (8, doc_ref.shape[1])))
         crow_ref[...] = c
@@ -92,8 +147,7 @@
             cn, rn = c[:, span], r[0:1, span]
             leave_ref[:, span] = jnp.where(rn == rn[:, -1:], jnp.exp2(cn[:, -1:] - cn), 0.0)
 
-    for copy in copies(step):
-        copy.wait()
+    wait(copies(step))
     late = []
     for g in range(GROUP):
         h = step * GROUP + g
@@ -112,6 +166,10 @@
         late.append((pass_ref, (pl.ds(h, 1), slice(None)), jnp.broadcast_to(total, (1, HD))))
     save(late)
 
+    @pl.when(step == steps - 1)
+    def _():
+        wait(following)
+
 
 def prepare_kernel(rrow_ref, crow_ref, enter_ref, mask_ref, cols_ref):
     sub = lax.broadcasted_iota(jnp.int32, (CHUNK, CHUNK), 0)
@@ -137,26 +195,24 @@
 
 
 def inside_kernel(
-    chunks, first, steps, crow_ref, cols_ref, mask_ref, k_ref, v_ref, gain_ref, q_hbm, gate_ref,
-    grad_ref, *refs,
+    chunks, first, steps, crow_ref, cols_ref, mask_ref, k_ref, v_ref, gain_ref, q_hbm, gate_hbm,
+    grad_hbm, *refs,
 ):
-    attn_ref, gnorm_ref, q_ref, turned_q_ref, probs_ref, sems = refs[-6:]
-    step = pl.program_id(0)
-
-    def copy(at):
-        here = head_span(first + at)
-        return pltpu.make_async_copy(q_hbm.at[:, here], q_ref.at[:, here], sems.at[at])
-
-    @pl.when(step == 0)
-    def _():
-        for at in range(steps):
-            copy(at).start()
-
-    cols_now = turned(cols_ref, first + step)
-    copy(step).wait()
+    q_ref, gate_ring, grad_ring, attn_ref, gnorm_ref, turned_q_ref, probs_ring, probs_hbm, sems = (
+        refs[-9:]
+    )
+    step = first + pl.program_id(0)
+    slot = step % 2
+    fetches = fetch_gates(step + 1, gate_hbm, grad_hbm, gate_ring, grad_ring, sems)
+    fetches += fetch_q(step + 1, q_hbm, q_ref, sems.at[2])
+    puts = put_probs(step - 1, probs_ring, probs_hbm, sems.at[3])
+    pl.when(step + 1 < steps)(lambda: start(fetches))
+    pl.when(step > 0)(lambda: start(puts))
+
+    cols_now = turned(cols_ref, step * RING)
     late = []
-    for g in range(1):
-        h = first + step
+    for g in range(RING):
+        h = step * RING + g
         cols = slice(g * HD, (g + 1) * HD)
         mine = head_span(h)
         for n, span in enumerate(spans(chunks)):
@@ -165,25 +221,32 @@
             c_row = crow_ref[pl.ds(h, 1), span]
             probs = decayed(scores, spread(cols_now[span], g), c_row, mask_ref.at[n])
             inside = dot(probs, v_ref[span, mine])
-            sig = sigmoid(gate_ref[span, cols].astype(F32))
-            gnorm = grad_ref[span, cols].astype(F32) * sig * gain_ref[0:1, cols]
+            sig = sigmoid(gate_ring[slot, span, cols].astype(F32))
+            gnorm = grad_ring[slot, span, cols].astype(F32) * sig * gain_ref[0:1, mine]
             save(late)
             late = [
-                (probs_ref, (g, n), probs),
+                (probs_ring, (slot, g, n), probs),
                 (attn_ref, (span, mine), inside),
                 (turned_q_ref, (h, slice(None), span), q.T),
                 (gnorm_ref, (span, mine), gnorm.astype(BF16)),
             ]
     save(late)
-
-
-def outside_kernel(chunks, entering, inputs, cols_ref, enter_ref, q_ref, gnorm_ref, loc_ref, *refs):
+    pl.when(step + 1 < steps)(lambda: wait(fetches))
+    pl.when(step > 0)(lambda: wait(puts))
+
+
+def outside_kernel(chunks, last, entering, inputs, cols_ref, enter_ref, q_ref, gnorm_ref, loc_ref, *refs):
     in_refs = refs[:inputs]
-    inside_ref, attn_ref, held_ref, sums_ref, sq_ref, inner_ref = refs[inputs:]
+    probs_ring, inside_ref, _, attn_ref, probs_hbm, held_ref, sums_ref, sq_ref, inner_ref, sem = (
+        refs[inputs:]
+    )
     step = pl.program_id(0)
+    steps = pl.num_programs(0)
+    puts = put_probs(last, probs_ring, probs_hbm, sem.at[0])
 
     @pl.when(step == 0)
     def _():
+        start(puts)
         sq_ref[...] = jnp.zeros_like(sq_ref)
         inner_ref[...] = jnp.zeros_like(inner_ref)
 
@@ -209,19 +272,24 @@
         late += [(sq_ref, (span, slice(None)), squares), (inner_ref, (span, slice(None)), inners)]
     save(late)
 
-    @pl.when(step == pl.num_programs(0) - 1)
+    @pl.when(step == steps - 1)
     def _():
+        wait(puts)
         sums_ref[0:1, :] = jnp.sum(sq_ref[...].T, axis=0, keepdims=True)
         sums_ref[1:2, :] = jnp.sum(inner_ref[...].T, axis=0, keepdims=True)
 
 
 def grad_kernel(chunks, parts, enter_ref, *refs):
-    turned_q_ref, gnorm_ref, attn_ref = refs[parts : parts + 3]
-    agrad_ref, turned_ref, bloc_ref, back_ref, alpha_ref, beta_ref = refs[parts + 3 :]
+    turned_q_ref, gnorm_ref, attn_ref, gate_hbm, grad_hbm, probs_hbm = refs[parts : parts + 6]
+    agrad_ref, turned_ref, bloc_ref, back_ref, alpha_ref = refs[parts + 6 : parts + 11]
+    gate_ring, grad_ring, probs_ring, beta_ref, sems = refs[parts + 11 :]
     step = pl.program_id(0)
+    following = fetch_gates(0, gate_hbm, grad_hbm, gate_ring, grad_ring, sems)
+    following += fetch_probs(0, probs_hbm, probs_ring, sems.at[2])
 
     @pl.when(step == 0)
     def _():
+        start(following)
         sums = refs[0][...]
         for ref in refs[1:parts]:
             sums = sums + ref[...]
@@ -251,17 +319,29 @@
         late.append((back_ref, h, back))
     save(late)
 
+    @pl.when(step == pl.num_programs(0) - 1)
+    def _():
+        wait(following)
+
 
 def inner_grad_kernel(
-    chunks, first, crow_ref, alpha_ref, cols_ref, mask_ref, k_ref, v_ref, attn_ref, held_ref,
-    agrad_ref, turned_q_ref, turned_agrad_ref, gain_ref, gate_ref, grad_ref, probs_ref, *refs,
+    chunks, first, steps, crow_ref, alpha_ref, cols_ref, mask_ref, k_ref, v_ref, attn_ref,
+    held_ref, agrad_ref, turned_q_ref, turned_agrad_ref, gain_ref, gate_hbm, grad_hbm, probs_hbm,
+    *refs,
 ):
-    dk_ref, dv_ref, dq_ref, gated_ref, ggate_ref = refs[-5:]
-    step = pl.program_id(0)
-    cols_now = turned(cols_ref, first + step)
+    dk_ref, dv_ref, gate_ring, grad_ring, probs_ring, out_ring, *outs_hbm, sems = refs[-10:]
+    step = first + pl.program_id(0)
+    slot = step % 2
+    fetches = fetch_gates(step + 1, gate_hbm, grad_hbm, gate_ring, grad_ring, sems)
+    fetches += fetch_probs(step + 1, probs_hbm, probs_ring, sems.at[2])
+    puts = put_outs(step - 1, out_ring, outs_hbm, sems.at[pl.ds(3, 3)])
+    pl.when(step + 1 < steps)(lambda: start(fetches))
+    pl.when(step > 0)(lambda: start(puts))
+
+    cols_now = turned(cols_ref, step * RING)
     late = []
-    for g in range(1):
-        h = first + step
+    for g in range(RING):
+        h = step * RING + g
         cols = slice(g * HD, (g + 1) * HD)
         mine = head_span(h)
         for n, span in enumerate(spans(chunks)):
@@ -271,27 +351,33 @@
             dscore = decayed(both[:, :CHUNK], spread(cols_now[span], g), c_row, mask_ref.at[n])
             enter = spread(cols_now[span], crow_ref.shape[0] + g)
             dq = dot(dscore, k) + enter * both[:, CHUNK:]
-            dv = dot(turned_agrad_ref[h, :, span], probs_ref[g, n])
+            dv = dot(turned_agrad_ref[h, :, span], probs_ring[slot, g, n])
             dk = dot(turned_q_ref[h, :, span], dscore)
-            normed = attn_ref[span, mine] * alpha_ref[span, :] * gain_ref[0:1, cols]
-            sig = sigmoid(gate_ref[span, cols].astype(F32))
+            normed = attn_ref[span, mine] * alpha_ref[span, :] * gain_ref[0:1, mine]
+            sig = sigmoid(gate_ring[slot, span, cols].astype(F32))
             gated = normed * sig
-            ggate = grad_ref[span, cols].astype(F32) * gated * (1.0 - sig)
+            ggate = grad_ring[slot, span, cols].astype(F32) * gated * (1.0 - sig)
             save(late)
             late = [
-                (dq_ref, (span, cols), dq.astype(BF16)),
+                (out_ring, (slot, 0, span, cols), dq.astype(BF16)),
                 (dv_ref, (h, slice(None), span), dv.astype(BF16)),
                 (dk_ref, (h, slice(None), span), dk.astype(BF16)),
-                (gated_ref, (span, cols), gated.astype(BF16)),
-                (ggate_ref, (span, cols), ggate.astype(BF16)),
+                (out_ring, (slot, 1, span, cols), gated.astype(BF16)),
+                (out_ring, (slot, 2, span, cols), ggate.astype(BF16)),
             ]
     save(late)
-
-
-def outer_grad_kernel(chunks, entering, inputs, enter_ref, leave_ref, k_ref, v_ref, *refs):
+    pl.when(step + 1 < steps)(lambda: wait(fetches))
+    pl.when(step > 0)(lambda: wait(puts))
+
+
+def outer_grad_kernel(chunks, last, entering, inputs, enter_ref, leave_ref, k_ref, v_ref, *refs):
     in_refs = refs[:inputs]
-    dkin_ref, dvin_ref, bloc_ref, dk_ref, dv_ref = refs[inputs:]
+    dkin_ref, dvin_ref, bloc_ref, out_ring = refs[inputs : inputs + 4]
+    dk_ref, dv_ref, *outs_hbm, sems = refs[inputs + 7 :]
     step = pl.program_id(0)
+    steps = pl.num_programs(0)
+    puts = put_outs(last, out_ring, outs_hbm, sems)
+    pl.when(step == 0)(lambda: start(puts))
     late = []
     for g in range(GROUP):
         h = step * GROUP + g
@@ -312,6 +398,7 @@
                 (dv_ref, (span, cols), dv.astype(BF16).T),
             ]
     save(late)
+    pl.when(step == steps - 1)(lambda: wait(puts))
 
 
 def hbm(x):
@@ -331,7 +418,7 @@
     out_ref[...] = a_ref[...] + b_ref[...]
 
 
-def call(kernel, grid, ins, outs, scratch=(), aliases=None, room=8, flops=0, moved=0, exps=0):
+def call(kernel, grid, ins, outs, scratch=(), aliases=None, room=4, flops=0, moved=0, exps=0):
     return pl.pallas_call(
         kernel,
         grid=grid,
@@ -465,7 +552,7 @@
     other, beside_pass = lax.optimization_barrier((other, beside_pass, fill(0, state)))[:2]
     to_x, to_y, chip_pass = call(
         functools.partial(pair_kernel, reverse), (),
-        kept(state, other, own_pass, beside_pass), [part, part, keep((heads, HD), F32)], room=2,
+        kept(state, other, own_pass, beside_pass), [part, part, keep((heads, HD), F32)], room=ROOM,
     )
 
     from_x, from_y = across(to_x, 2), across(to_y, 4)
@@ -475,7 +562,7 @@
     )[:4]
     row, sent = call(
         functools.partial(row_kernel, reverse), (),
-        kept(to_x, to_y, from_x, from_y, chip_pass, x_pass, far_pass), [part, part], room=2,
+        kept(to_x, to_y, from_x, from_y, chip_pass, x_pass, far_pass), [part, part], room=ROOM,
     )
 
     row_in, sent_in = across(row, 4), across(sent, 2)
@@ -483,7 +570,7 @@
     (ahead,) = call(
         functools.partial(ahead_kernel, reverse), (),
         kept(from_x, from_y, row_in, sent_in, x_pass, far_pass),
-        [keep((2 * quarter, HD, HD), F32)], room=2,
+        [keep((2 * quarter, HD, HD), F32)], room=ROOM,
     )
 
     beside = across(ahead, 1)
@@ -536,16 +623,14 @@
     whole = lambda *dims: pl.BlockSpec(dims, lambda i: (0,) * len(dims))
     anywhere = pl.BlockSpec(memory_space=pl.ANY)
 
-    def wide(base=0, group=1):
-        return pl.BlockSpec((rows, group * HD), lambda i: (0, i + base // group))
-
-    def gain_spec(base=0):
-        return pl.BlockSpec((1, HD), lambda i: (0, i + base))
-
-    probs_spec = pl.BlockSpec((1, chunks, CHUNK, CHUNK), lambda i: (i, 0, 0, 0))
     by_head = (heads, HD, rows)
     local_dims = (heads, chunks, HD, HD)
-    wide_shape = pltpu.HBM((rows, cols), BF16)
+    wide_out = (pltpu.HBM((rows, cols), BF16), anywhere)
+    probs_out = (pltpu.HBM((heads, chunks, CHUNK, CHUNK), BF16), anywhere)
+    ring = keep((2, rows, RING * HD), BF16)
+    probs_ring = keep((2, RING, chunks, CHUNK, CHUNK), BF16)
+    out_ring = keep((2, 3, rows, RING * HD), BF16)
+    sems = pltpu.SemaphoreType.DMA
     queries, key_rows, value_rows, gate_input, out_grad = map(
         hbm, (queries, key_rows, value_rows, gate_input, out_grad)
     )
@@ -554,126 +639,129 @@
 
     by_token = (rows, cols)
     steps = heads // GROUP
-    crow, enter, leave, rrow, keys, values, local, state, own_pass = call(
+    (
+        crow, enter, leave, rrow, keys, values, local, state, own_pass, gain, kept_q, *rings
+    ) = call(
         functools.partial(state_kernel, chunks, steps),
         grid,
         [
-            (hbm(log_decay), whole(heads, rows)), (hbm(doc_row), whole(1, rows)),
-            (key_rows, anywhere), (value_rows, anywhere),
+            (hbm(x), anywhere)
+            for x in (
+                log_decay, doc_row, gain_row, key_rows, value_rows, queries, gate_input, out_grad
+            )
         ],
         [keep((heads, rows), F32)] * 3
         + [
             keep((8, rows), F32), keep(by_token, BF16), keep(by_token, BF16),
             keep(local_dims, F32), keep((heads, HD, HD), F32), keep((heads, HD), F32),
+            keep((1, cols), F32), keep(by_token, BF16), ring, ring,
         ],
-        [pltpu.SemaphoreType.DMA((2, steps))],
-        flops=small, moved=2 * big,
+        [
+            pltpu.VMEM((heads, rows), F32), pltpu.VMEM((1, rows), jnp.int32),
+            sems((2, steps)), sems((3,)), sems((3,)),
+        ],
+        room=ROOM, flops=small, moved=2 * big,
     )
 
     ready = []
-    made = []
-    probs = []
+    made = [kept_q, *rings]
 
     def fill_forward(window, tie):
-        base = window * share
         if not ready:
             ready[:] = call(
                 prepare_kernel, (), kept(after(rrow, tie), crow, enter),
                 [keep((chunks, CHUNK, CHUNK), F32), keep((rows, HD), F32)],
-                flops=8 * rows * CHUNK,
+                room=ROOM, flops=8 * rows * CHUNK,
             )
         mask, columns = ready
-        ins = kept(after(crow, tie), columns, mask, keys, values) + [
-            (hbm(gain_row), gain_spec(base)), (queries, anywhere), (gate_input, wide(base)),
-            (out_grad, wide(base)),
-        ]
+        ins = kept(after(crow, tie), columns, mask, keys, values, gain)
+        ins += [(x, anywhere) for x in (queries, gate_input, out_grad)]
         aliases = {len(ins) + i: i for i in range(len(made))}
-        ins += kept(*made)
-        *made[:], fresh = call(
-            functools.partial(inside_kernel, chunks, base, share),
-            (share,),
+        ins += kept(*made[:7]) + [(hbm(x), anywhere) for x in made[7:]]
+        made[:] = call(
+            functools.partial(inside_kernel, chunks, window * share // RING, heads // RING),
+            (share // RING,),
             ins,
             [
-                keep(by_token, F32), keep(by_token, BF16), keep(by_token, BF16),
-                keep(by_head, BF16),
-                (pltpu.HBM((share, chunks, CHUNK, CHUNK), BF16), probs_spec),
+                keep(by_token, BF16), ring, ring, keep(by_token, F32), keep(by_token, BF16),
+                keep(by_head, BF16), probs_ring, probs_out,
             ],
-            [pltpu.SemaphoreType.DMA((share,))],
-            aliases=aliases, room=6,
+            [sems((4,))],
+            aliases=aliases, room=ROOM,
             flops=2 * tile // WINDOWS, moved=5 * big // WINDOWS,
             exps=rows * (CHUNK + HD) * heads // WINDOWS,
         )
-        probs.append(fresh)
-        return fresh
+        return made[7]
 
     entering, incoming, passes = scan_devices(state, own_pass, None, fill_forward, False)
     mask, columns = ready
-    inside, gnorm, kept_q, turned_q = made
+    kept_q, _, _, inside, gnorm, turned_q, probs_ringed, probs = made
     tall = pltpu.VMEM((rows, HD), F32)
 
-    attn, held, sums = call(
-        functools.partial(outside_kernel, chunks, entering, len(incoming)),
+    attn, probs, held, sums = call(
+        functools.partial(outside_kernel, chunks, heads // RING - 1, entering, len(incoming)),
         grid,
-        kept(columns, enter, kept_q, gnorm, local, *incoming, inside),
-        [keep(by_token, F32), keep(local_dims, BF16), keep((2, rows), F32)],
-        [tall, tall],
-        {5 + len(incoming): 0},
-        flops=small, moved=big,
+        kept(columns, enter, kept_q, gnorm, local, *incoming, probs_ringed, inside)
+        + [(hbm(probs), anywhere)],
+        [keep(by_token, F32), probs_out, keep(local_dims, BF16), keep((2, rows), F32)],
+        [tall, tall, sems((1,))],
+        {6 + len(incoming): 0, 7 + len(incoming): 1},
+        room=ROOM, flops=small, moved=big,
     )
 
     apart = 1
     while apart < parts // 2:
         other_sums = lax.ppermute(sums, "head", [(i, i ^ apart) for i in range(parts)])
-        (sums,) = call(add_kernel, (), kept(sums, other_sums), [keep((2, rows), F32)], room=2)
+        (sums,) = call(add_kernel, (), kept(sums, other_sums), [keep((2, rows), F32)], room=ROOM)
         apart *= 2
     other_sums = lax.ppermute(sums, "head", [(i, i ^ apart) for i in range(parts)])
 
-    agrad, turned_agrad, bloc, back, alpha, _ = call(
+    agrad, turned_agrad, bloc, back, alpha, *rings = call(
         functools.partial(grad_kernel, chunks, 2),
         grid,
-        kept(enter, sums, other_sums, turned_q, gnorm, attn),
+        kept(enter, sums, other_sums, turned_q, gnorm, attn)
+        + [(hbm(x), anywhere) for x in (gate_input, out_grad, probs)],
         [
             keep(by_token, BF16), keep(by_head, BF16), keep(local_dims, F32),
-            keep((heads, HD, HD), F32), keep((rows, HD), F32), keep((rows, HD), F32),
+            keep((heads, HD, HD), F32), keep((rows, HD), F32), ring, ring, probs_ring,
         ],
-        flops=small, moved=big,
-    )
-
-    inner = [turned_q, turned_agrad]
-    outs = []
+        [tall, sems((3,))],
+        room=ROOM, flops=small, moved=big,
+    )
+
+    inner = [turned_q, turned_agrad, *rings]
 
     def fill_backward(window, tie):
-        base = window * share
         ins = kept(
-            after(crow, tie), alpha, columns, mask, keys, values, attn, held, agrad, *inner
+            after(crow, tie), alpha, columns, mask, keys, values, attn, held, agrad, *inner[:2], gain
         )
-        aliases = {len(ins) - 2: 0, len(ins) - 1: 1}
-        ins += [
-            (hbm(gain_row), gain_spec(base)), (gate_input, wide(base)), (out_grad, wide(base)),
-            (hbm(probs[window]), probs_spec),
-        ]
-        aliases.update({len(ins) + i: 2 + i for i in range(len(outs))})
-        ins += [(hbm(x), anywhere) for x in outs]
-        inner[0], inner[1], *outs[:] = call(
-            functools.partial(inner_grad_kernel, chunks, base),
-            (share,),
+        ins += [(hbm(x), anywhere) for x in (gate_input, out_grad, probs)]
+        aliases = {9: 0, 10: 1}
+        aliases.update({len(ins) - 2 + i: i for i in range(2, len(inner))})
+        ins += kept(*inner[2:6]) + [(hbm(x), anywhere) for x in inner[6:]]
+        inner[:] = call(
+            functools.partial(inner_grad_kernel, chunks, window * share // RING, heads // RING),
+            (share // RING,),
             ins,
-            [keep(by_head, BF16)] * 2 + [(wide_shape, wide(base))] * 3,
-            aliases=aliases, room=6,
+            [keep(by_head, BF16)] * 2 + [ring, ring, probs_ring, out_ring] + [wide_out] * 3,
+            [sems((6,))],
+            aliases=aliases, room=ROOM,
             flops=(4 * tile + small) // WINDOWS, moved=7 * big // WINDOWS,
             exps=rows * (CHUNK + HD) * heads // WINDOWS,
         )
-        return outs[0]
+        return inner[6]
 
     entering, outgoing, _ = scan_devices(back, own_pass, passes, fill_backward, True)
-    dq, gated, gate_grad = outs
-
-    dk, dv = call(
-        functools.partial(outer_grad_kernel, chunks, entering, len(outgoing)),
+    wide = pl.BlockSpec((rows, GROUP * HD), lambda i: (0, i))
+    dk, dv, dq, gated, gate_grad = call(
+        functools.partial(outer_grad_kernel, chunks, heads // RING - 1, entering, len(outgoing)),
         grid,
-        kept(enter, leave, keys, values, *outgoing, *inner, bloc),
-        [(wide_shape, wide(0, GROUP))] * 2,
-        flops=2 * small, moved=2 * big,
+        kept(enter, leave, keys, values, *outgoing, *inner[:2], bloc, inner[5])
+        + [(hbm(x), anywhere) for x in inner[6:]],
+        [(pltpu.HBM((rows, cols), BF16), wide)] * 2 + [wide_out] * 3,
+        [sems((3,))],
+        {8 + len(outgoing) + i: 2 + i for i in range(3)},
+        room=ROOM, flops=2 * small, moved=2 * big,
     )
     return (gated, gate_grad, dq, dk, dv)
 

time: 110 us -> 101 us (0.918)
  Pallas kernels: 86 us -> 75.2 us
  waiting for transfers between devices: 4.69 us -> 6.7 us
    pallas_call x20, Pallas kernels: 86 us -> 75.2 us  [call(): pl.pallas_call(kernel, grid=grid, in_specs=[spec for _, spec in ins], out...]
    ppermute x15, waiting for transfers between devices: 0.65 us -> 2.68 us  [across(): return lax.ppermute(x, 'seq', [(i, i ^ flips) for i in range(devices)])]
  transfers between devices with their start and end apart: 17 -> 17, of which waited for: 3 -> 6; matrix products, arithmetic and copies ran while one was open for 0% -> 0% of each run, Pallas kernels for 53% -> 45%
where the time goes in v2:
time: 101 us; the launch traced here: 100 us
  Pallas kernels  75.2 us (74%)
  starting transfers between devices  17.3 us (17%)
  waiting for transfers between devices  6.7 us (7%)
  between operations  1.04 us (1%)
    pallas_call x20, Pallas kernels, call(): pl.pallas_call(kernel, grid=grid, in_specs=[spec for _, spec in ins], out...  75.2 us
    ppermute x15, starting transfers between devices, across(): return lax.ppermute(x, 'seq', [(i, i ^ flips) for i in range(devices)])  13.1 us
    ppermute x2, starting transfers between devices, body(): lax.ppermute(sums, 'head', [(i, i ^ apart) for i in range(parts)])  4.24 us
    ppermute x2, waiting for transfers between devices, body(): lax.ppermute(sums, 'head', [(i, i ^ apart) for i in range(parts)])  4.02 us
    ppermute x15, waiting for transfers between devices, across(): return lax.ppermute(x, 'seq', [(i, i ^ flips) for i in range(devices)])  2.68 us
  transfers between devices with their start and end apart: 17, of which 6 were waited for; matrix products, arithmetic and copies ran while one was open for 0% of the time, Pallas kernels for 45%

profile of v2, /device:TPU:0, one launch (start us, length us, event | category | flops | bytes accessed | tf_op | source)
XLA Modules:
  0.0 100.3 jit_solution(14667019847858112986)
XLA Ops:
  0.6 8.5 %shard_map.119 = (f32[16,1024]{1,0:T(8,128)S(1)}, f32[16,1024]{1,0:T(8,128)S(1)}, f32[16,1024]{1,0:T(8,128)S(1)}, f32[8,1024]{1,0:T(8,128)S(1)}, bf16[1024,2048]...) custom-call(f32[16,1024]{1,0:T(8,128)} %lc_hbm.1, ...), custom_call_target="tpu_custom_call" | custom-call | flops 536870912 | bytes 8388608 | tf_op jit(solution)/shard_map/pallas_call | solution.py:422
  10.0 4.6 %shard_map.121 = (bf16[1024,2048]{1,0:T(8,128)(2,1)S(1)}, bf16[2,1024,128]{2,1,0:T(8,128)(2,1)S(1)}, bf16[2,1024,128]{2,1,0:T(8,128)(2,1)S(1)}, f32[1024,2048]{1...) custom-call(f32[16,1024]{1,0:T(8,128)S(1)} %get-tuple-element.247.cr, ...), custom_call_target="tpu_custom_call", output_to_operand_aliasing={{0}: (9, {}), {1}: (10, {}), {2}: (11, {})} | custom-call | flops 536870912 | bytes 5242880 | tf_op jit(solution)/shard_map/pallas_call | solution.py:422
  14.8 3.0 %collective-permute-start.2 = (f32[4,128,128]{2,1,0:T(8,128)S(1)}, f32[4,128,128]{2,1,0:T(8,128)S(1)}, u32[]{:S(2)}, u32[]{:S(2)}) collective-permute-start(f32[4,128,128]{2,1,0:T(8,128)S(1)} %get-tuple-element.156.to_x_ref), channel_id=1, source_target_pairs={{0,8},{4,12},{8,0},{12,4},{16,24},{20,28},{24,16},{28,20},{1,9},{5... | collective-permute-start | bytes 786440 | tf_op jit(solution)/shard_map/ppermute | solution.py:442
  17.8 1.5 %collective-permute-start.3 = (f32[4,128,128]{2,1,0:T(8,128)S(1)}, f32[4,128,128]{2,1,0:T(8,128)S(1)}, u32[]{:S(2)}, u32[]{:S(2)}) collective-permute-start(f32[4,128,128]{2,1,0:T(8,128)S(1)} %get-tuple-element.157.to_y_ref), channel_id=1, source_target_pairs={{0,16},{4,20},{8,24},{12,28},{16,0},{20,4},{24,8},{28,12},{1,17},{... | collective-permute-start | bytes 786440 | tf_op jit(solution)/shard_map/ppermute | solution.py:442
  19.4 1.9 %collective-permute-start.4 = (f32[16,128]{1,0:T(8,128)S(1)}, f32[16,128]{1,0:T(8,128)S(1)}, u32[]{:S(2)}, u32[]{:S(2)}) collective-permute-start(f32[16,128]{1,0:T(8,128)S(1)} %get-tuple-element.158.chip_ref), channel_id=1, source_target_pairs={{0,8},{4,12},{8,0},{12,4},{16,24},{20,28},{24,16},{28,20},{1,9},{5... | collective-permute-start | bytes 24584 | tf_op jit(solution)/shard_map/ppermute | solution.py:442
  21.3 4.6 %shard_map.123 = (bf16[1024,2048]{1,0:T(8,128)(2,1)S(1)}, bf16[2,1024,128]{2,1,0:T(8,128)(2,1)S(1)}, bf16[2,1024,128]{2,1,0:T(8,128)(2,1)S(1)}, f32[1024,2048]{1...) custom-call(f32[16,1024]{1,0:T(8,128)S(1)} %get-tuple-element.247.cr, ...), custom_call_target="tpu_custom_call", output_to_operand_aliasing={{0}: (9, {}), {1}: (10, {}), {2}: (11, {}), {3}: (12, {}), ... | custom-call | flops 536870912 | bytes 5242880 | tf_op jit(solution)/shard_map/pallas_call | solution.py:422
  26.1 1.6 %collective-permute-start.6 = (f32[4,128,128]{2,1,0:T(8,128)S(1)}, f32[4,128,128]{2,1,0:T(8,128)S(1)}, u32[]{:S(2)}, u32[]{:S(2)}) collective-permute-start(f32[4,128,128]{2,1,0:T(8,128)S(1)} %get-tuple-element.172), channel_id=1, source_target_pairs={{0,16},{4,20},{8,24},{12,28},{16,0},{20,4},{24,8},{28,12},{1,17},{... | collective-permute-start | bytes 786440 | tf_op jit(solution)/shard_map/ppermute | solution.py:442
  28.2 4.6 %shard_map.125 = (bf16[1024,2048]{1,0:T(8,128)(2,1)S(1)}, bf16[2,1024,128]{2,1,0:T(8,128)(2,1)S(1)}, bf16[2,1024,128]{2,1,0:T(8,128)(2,1)S(1)}, f32[1024,2048]{1...) custom-call(f32[16,1024]{1,0:T(8,128)S(1)} %get-tuple-element.247.cr, ...), custom_call_target="tpu_custom_call", output_to_operand_aliasing={{0}: (9, {}), {1}: (10, {}), {2}: (11, {}), {3}: (12, {}), ... | custom-call | flops 536870912 | bytes 5242880 | tf_op jit(solution)/shard_map/pallas_call | solution.py:422
  33.3 1.3 %collective-permute-done.7.sent_ref = f32[4,128,128]{2,1,0:T(8,128)S(1)} collective-permute-done((f32[4,128,128]{2,1,0:T(8,128)S(1)}, f32[4,128,128]{2,1,0:T(8,128)S(1)}, u32[]{:S(2)}, u32[]{:S(2)}) %collective-permute-start.7) | collective-permute-done | bytes 262176 | tf_op jit(solution)/shard_map/ppermute | solution.py:442
  34.7 4.6 %shard_map.127 = (bf16[1024,2048]{1,0:T(8,128)(2,1)S(1)}, bf16[2,1024,128]{2,1,0:T(8,128)(2,1)S(1)}, bf16[2,1024,128]{2,1,0:T(8,128)(2,1)S(1)}, f32[1024,2048]{1...) custom-call(f32[16,1024]{1,0:T(8,128)S(1)} %get-tuple-element.247.cr, ...), custom_call_target="tpu_custom_call", output_to_operand_aliasing={{0}: (9, {}), {1}: (10, {}), {2}: (11, {}), {3}: (12, {}), ... | custom-call | flops 536870912 | bytes 5242880 | tf_op jit(solution)/shard_map/pallas_call | solution.py:422
  39.3 7.8 %shard_map.128 = (f32[1024,2048]{1,0:T(8,128)S(1)}, bf16[16,4,256,256]{3,2,1,0:T(8,128)(2,1)}, bf16[16,4,128,128]{3,2,1,0:T(8,128)(2,1)S(1)}, f32[2,1024]{1,0:T(2,128)S(1)}) custom-call(f32[1024,128]{1,0:T(8,128)S(1)} %get-tuple-element.145.cols_ref, f32[16,1024]{1,0:T(8,128)S(1)} %get-tuple-element.137.enter_ref, ...), custom_call_target="tpu_custom_call", output_to_operand_aliasing={{0}: (10, {}), {1}: (11, {})} | custom-call | flops 536870912 | bytes 4194304 | tf_op jit(solution)/shard_map/pallas_call | solution.py:422
  47.2 1.7 %collective-permute-start.9 = (f32[2,1024]{1,0:T(2,128)S(1)}, f32[2,1024]{1,0:T(2,128)S(1)}, u32[]{:S(2)}, u32[]{:S(2)}) collective-permute-start(f32[2,1024]{1,0:T(2,128)S(1)} %get-tuple-element.200.a_ref), channel_id=1, source_target_pairs={{0,1},{1,0},{2,3},{3,2},{4,5},{5,4},{6,7},{7,6},{8,9},{9,8},{10,11... | collective-permute-start | bytes 24584 | tf_op jit(solution)/shard_map/ppermute | solution.py:714
  48.8 2.1 %collective-permute-done.9.b_ref = f32[2,1024]{1,0:T(2,128)S(1)} collective-permute-done((f32[2,1024]{1,0:T(2,128)S(1)}, f32[2,1024]{1,0:T(2,128)S(1)}, u32[]{:S(2)}, u32[]{:S(2)}) %collective-permute-start.9) | collective-permute-done | bytes 8224 | tf_op jit(solution)/shard_map/ppermute | solution.py:714
  50.9 2.6 %collective-permute-start.10 = (f32[2,1024]{1,0:T(2,128)S(1)}, f32[2,1024]{1,0:T(2,128)S(1)}, u32[]{:S(2)}, u32[]{:S(2)}) collective-permute-start(f32[2,1024]{1,0:T(2,128)S(1)} %shard_map.129.refs_0_), channel_id=1, source_target_pairs={{0,2},{1,3},{2,0},{3,1},{4,6},{5,7},{6,4},{7,5},{8,10},{9,11},{10,... | collective-permute-start | bytes 24584 | tf_op jit(solution)/shard_map/ppermute | solution.py:717
  53.5 2.0 %collective-permute-done.10.refs_1_ = f32[2,1024]{1,0:T(2,128)S(1)} collective-permute-done((f32[2,1024]{1,0:T(2,128)S(1)}, f32[2,1024]{1,0:T(2,128)S(1)}, u32[]{:S(2)}, u32[]{:S(2)}) %collective-permute-start.10) | collective-permute-done | bytes 8224 | tf_op jit(solution)/shard_map/ppermute | solution.py:717
  55.4 5.2 %shard_map.130 = (bf16[1024,2048]{1,0:T(8,128)(2,1)S(1)}, bf16[16,128,1024]{2,1,0:T(8,128)(2,1)S(1)}, f32[16,4,128,128]{3,2,1,0:T(8,128)S(1)}, f32[16,128,128]{2...) custom-call(f32[16,1024]{1,0:T(8,128)S(1)} %get-tuple-element.137.en, ...), custom_call_target="tpu_custom_call" | custom-call | flops 536870912 | bytes 4194304 | tf_op jit(solution)/shard_map/pallas_call | solution.py:422
  60.7 6.4 %shard_map.131 = (bf16[16,128,1024]{2,1,0:T(8,128)(2,1)S(1)}, bf16[16,128,1024]{2,1,0:T(8,128)(2,1)S(1)}, bf16[2,1024,128]{2,1,0:T(8,128)(2,1)S(1)}, bf16[2,1024...) custom-call(f32[16,1024]{1,0:T(8,128)S(1)} %get-tuple-element.247.cr, ...), custom_call_target="tpu_custom_call", output_to_operand_aliasing={{0}: (9, {}), {1}: (10, {}), {2}: (15, {}), {3}: (16, {}), ... | custom-call | flops 1207959552 | bytes 7340032 | tf_op jit(solution)/shard_map/pallas_call | solution.py:422
  67.2 0.8 collective-permute-start.12
  68.0 1.0 %collective-permute-start.13 = (f32[4,128,128]{2,1,0:T(8,128)S(1)}, f32[4,128,128]{2,1,0:T(8,128)S(1)}, u32[]{:S(2)}, u32[]{:S(2)}) collective-permute-start(f32[4,128,128]{2,1,0:T(8,128)S(1)} %get-tuple-element.217.to_y_ref), channel_id=1, source_target_pairs={{0,16},{4,20},{8,24},{12,28},{16,0},{20,4},{24,8},{28,12},{1,17},{... | collective-permute-start | bytes 786440 | tf_op jit(solution)/shard_map/ppermute | solution.py:442
  69.0 6.5 %shard_map.133 = (bf16[16,128,1024]{2,1,0:T(8,128)(2,1)S(1)}, bf16[16,128,1024]{2,1,0:T(8,128)(2,1)S(1)}, bf16[2,1024,128]{2,1,0:T(8,128)(2,1)S(1)}, bf16[2,1024...) custom-call(f32[16,1024]{1,0:T(8,128)S(1)} %get-tuple-element.247.cr, ...), custom_call_target="tpu_custom_call", output_to_operand_aliasing={{0}: (9, {}), {1}: (10, {}), {2}: (15, {}), {3}: (16, {}), ... | custom-call | flops 1207959552 | bytes 7340032 | tf_op jit(solution)/shard_map/pallas_call | solution.py:422
  76.7 1.1 %collective-permute-start.14 = (f32[4,128,128]{2,1,0:T(8,128)S(1)}, f32[4,128,128]{2,1,0:T(8,128)S(1)}, u32[]{:S(2)}, u32[]{:S(2)}) collective-permute-start(f32[4,128,128]{2,1,0:T(8,128)S(1)} %get-tuple-element.233), channel_id=1, source_target_pairs={{0,16},{4,20},{8,24},{12,28},{16,0},{20,4},{24,8},{28,12},{1,17},{... | collective-permute-start | bytes 786440 | tf_op jit(solution)/shard_map/ppermute | solution.py:442
  78.6 6.5 %shard_map.135 = (bf16[16,128,1024]{2,1,0:T(8,128)(2,1)S(1)}, bf16[16,128,1024]{2,1,0:T(8,128)(2,1)S(1)}, bf16[2,1024,128]{2,1,0:T(8,128)(2,1)S(1)}, bf16[2,1024...) custom-call(f32[16,1024]{1,0:T(8,128)S(1)} %get-tuple-element.247.cr, ...), custom_call_target="tpu_custom_call", output_to_operand_aliasing={{0}: (9, {}), {1}: (10, {}), {2}: (15, {}), {3}: (16, {}), ... | custom-call | flops 1207959552 | bytes 7340032 | tf_op jit(solution)/shard_map/pallas_call | solution.py:422
  85.3 6.6 %shard_map.137 = (bf16[16,128,1024]{2,1,0:T(8,128)(2,1)S(1)}, bf16[16,128,1024]{2,1,0:T(8,128)(2,1)S(1)}, bf16[2,1024,128]{2,1,0:T(8,128)(2,1)S(1)}, bf16[2,1024...) custom-call(f32[16,1024]{1,0:T(8,128)S(1)} %get-tuple-element.247.cr, ...), custom_call_target="tpu_custom_call", output_to_operand_aliasing={{0}: (9, {}), {1}: (10, {}), {2}: (15, {}), {3}: (16, {}), ... | custom-call | flops 1207959552 | bytes 7340032 | tf_op jit(solution)/shard_map/pallas_call | solution.py:422
  91.9 8.2 %shard_map.138 = (bf16[1024,2048]{1,0:T(8,128)(2,1)}, bf16[1024,2048]{1,0:T(8,128)(2,1)}, bf16[1024,2048]{1,0:T(8,128)(2,1)}, bf16[1024,2048]{1,0:T(8,128)(2,1)}, bf16[1024,2048]{1,0:T(8,128)(2,1)}) custom-call(f32[16,1024]{1,0:T(8,128)S(1)} %get-tuple-element.137.enter_ref, ...), custom_call_target="tpu_custom_call", output_to_operand_aliasing={{2}: (12, {}), {3}: (13, {}), {4}: (14, {})} | custom-call | flops 1073741824 | bytes 8388608 | tf_op jit(solution)/shard_map/pallas_call | solution.py:422
  (30 shorter events, 4.7 us)
Async XLA Ops:
  9.1 5.6 %collective-permute-start = (f32[16,128,128]{2,1,0:T(8,128)S(1)}, f32[16,128,128]{2,1,0:T(8,128)S(1)}, u32[]{:S(2)}, u32[]{:S(2)}) collective-permute-start(f32[16,128,128]{2,1,0:T(8,128)S(1)} %get-tuple-element.142.state_ref), channel_id=1, source_target_pairs={{0,4},{4,0},{8,12},{12,8},{16,20},{20,16},{24,28},{28,24},{1,5},{5... | collective-permute-start | bytes 3145736 | tf_op jit(solution)/shard_map/ppermute | solution.py:442
  9.6 5.0 %collective-permute-start.1 = (f32[16,128]{1,0:T(8,128)S(1)}, f32[16,128]{1,0:T(8,128)S(1)}, u32[]{:S(2)}, u32[]{:S(2)}) collective-permute-start(f32[16,128]{1,0:T(8,128)S(1)} %get-tuple-element.146.pass_ref), channel_id=1, source_target_pairs={{0,4},{4,0},{8,12},{12,8},{16,20},{20,16},{24,28},{28,24},{1,5},{5... | collective-permute-start | bytes 24584 | tf_op jit(solution)/shard_map/ppermute | solution.py:442
  14.8 11.1 %collective-permute-start.2 = (f32[4,128,128]{2,1,0:T(8,128)S(1)}, f32[4,128,128]{2,1,0:T(8,128)S(1)}, u32[]{:S(2)}, u32[]{:S(2)}) collective-permute-start(f32[4,128,128]{2,1,0:T(8,128)S(1)} %get-tuple-element.156.to_x_ref), channel_id=1, source_target_pairs={{0,8},{4,12},{8,0},{12,4},{16,24},{20,28},{24,16},{28,20},{1,9},{5... | collective-permute-start | bytes 786440 | tf_op jit(solution)/shard_map/ppermute | solution.py:442
  17.8 8.2 %collective-permute-start.3 = (f32[4,128,128]{2,1,0:T(8,128)S(1)}, f32[4,128,128]{2,1,0:T(8,128)S(1)}, u32[]{:S(2)}, u32[]{:S(2)}) collective-permute-start(f32[4,128,128]{2,1,0:T(8,128)S(1)} %get-tuple-element.157.to_y_ref), channel_id=1, source_target_pairs={{0,16},{4,20},{8,24},{12,28},{16,0},{20,4},{24,8},{28,12},{1,17},{... | collective-permute-start | bytes 786440 | tf_op jit(solution)/shard_map/ppermute | solution.py:442
  19.3 6.6 %collective-permute-start.5 = (f32[16,128]{1,0:T(8,128)S(1)}, f32[16,128]{1,0:T(8,128)S(1)}, u32[]{:S(2)}, u32[]{:S(2)}) collective-permute-start(f32[16,128]{1,0:T(8,128)S(1)} %get-tuple-element.158.chip_ref), channel_id=1, source_target_pairs={{0,24},{4,28},{8,16},{12,20},{16,8},{20,12},{24,0},{28,4},{1,25},{... | collective-permute-start | bytes 24584 | tf_op jit(solution)/shard_map/ppermute | solution.py:442
  19.4 6.6 %collective-permute-start.4 = (f32[16,128]{1,0:T(8,128)S(1)}, f32[16,128]{1,0:T(8,128)S(1)}, u32[]{:S(2)}, u32[]{:S(2)}) collective-permute-start(f32[16,128]{1,0:T(8,128)S(1)} %get-tuple-element.158.chip_ref), channel_id=1, source_target_pairs={{0,8},{4,12},{8,0},{12,4},{16,24},{20,28},{24,16},{28,20},{1,9},{5... | collective-permute-start | bytes 24584 | tf_op jit(solution)/shard_map/ppermute | solution.py:442
  26.1 7.2 %collective-permute-start.6 = (f32[4,128,128]{2,1,0:T(8,128)S(1)}, f32[4,128,128]{2,1,0:T(8,128)S(1)}, u32[]{:S(2)}, u32[]{:S(2)}) collective-permute-start(f32[4,128,128]{2,1,0:T(8,128)S(1)} %get-tuple-element.172), channel_id=1, source_target_pairs={{0,16},{4,20},{8,24},{12,28},{16,0},{20,4},{24,8},{28,12},{1,17},{... | collective-permute-start | bytes 786440 | tf_op jit(solution)/shard_map/ppermute | solution.py:442
  27.7 6.9 %collective-permute-start.7 = (f32[4,128,128]{2,1,0:T(8,128)S(1)}, f32[4,128,128]{2,1,0:T(8,128)S(1)}, u32[]{:S(2)}, u32[]{:S(2)}) collective-permute-start(f32[4,128,128]{2,1,0:T(8,128)S(1)} %get-tuple-element.173), channel_id=1, source_target_pairs={{0,8},{4,12},{8,0},{12,4},{16,24},{20,28},{24,16},{28,20},{1,9},{5... | collective-permute-start | bytes 786440 | tf_op jit(solution)/shard_map/ppermute | solution.py:442
  34.6 4.7 %collective-permute-start.8 = (f32[8,128,128]{2,1,0:T(8,128)S(1)}, f32[8,128,128]{2,1,0:T(8,128)S(1)}, u32[]{:S(2)}, u32[]{:S(2)}) collective-permute-start(f32[8,128,128]{2,1,0:T(8,128)S(1)} %shard_map.126.refs_0_), channel_id=1, source_target_pairs={{0,4},{4,0},{8,12},{12,8},{16,20},{20,16},{24,28},{28,24},{1,5},{5... | collective-permute-start | bytes 1572872 | tf_op jit(solution)/shard_map/ppermute | solution.py:442
  47.2 3.7 %collective-permute-start.9 = (f32[2,1024]{1,0:T(2,128)S(1)}, f32[2,1024]{1,0:T(2,128)S(1)}, u32[]{:S(2)}, u32[]{:S(2)}) collective-permute-start(f32[2,1024]{1,0:T(2,128)S(1)} %get-tuple-element.200.a_ref), channel_id=1, source_target_pairs={{0,1},{1,0},{2,3},{3,2},{4,5},{5,4},{6,7},{7,6},{8,9},{9,8},{10,11... | collective-permute-start | bytes 24584 | tf_op jit(solution)/shard_map/ppermute | solution.py:714
  50.9 4.5 %collective-permute-start.10 = (f32[2,1024]{1,0:T(2,128)S(1)}, f32[2,1024]{1,0:T(2,128)S(1)}, u32[]{:S(2)}, u32[]{:S(2)}) collective-permute-start(f32[2,1024]{1,0:T(2,128)S(1)} %shard_map.129.refs_0_), channel_id=1, source_target_pairs={{0,2},{1,3},{2,0},{3,1},{4,6},{5,7},{6,4},{7,5},{8,10},{9,11},{10,... | collective-permute-start | bytes 24584 | tf_op jit(solution)/shard_map/ppermute | solution.py:717
  60.6 6.5 %collective-permute-start.11 = (f32[16,128,128]{2,1,0:T(8,128)S(1)}, f32[16,128,128]{2,1,0:T(8,128)S(1)}, u32[]{:S(2)}, u32[]{:S(2)}) collective-permute-start(f32[16,128,128]{2,1,0:T(8,128)S(1)} %get-tuple-element.204.state_ref), channel_id=1, source_target_pairs={{0,4},{4,0},{8,12},{12,8},{16,20},{20,16},{24,28},{28,24},{1,5},{5... | collective-permute-start | bytes 3145736 | tf_op jit(solution)/shard_map/ppermute | solution.py:442
  67.2 8.7 %collective-permute-start.12 = (f32[4,128,128]{2,1,0:T(8,128)S(1)}, f32[4,128,128]{2,1,0:T(8,128)S(1)}, u32[]{:S(2)}, u32[]{:S(2)}) collective-permute-start(f32[4,128,128]{2,1,0:T(8,128)S(1)} %get-tuple-element.216.to_x_ref), channel_id=1, source_target_pairs={{0,8},{4,12},{8,0},{12,4},{16,24},{20,28},{24,16},{28,20},{1,9},{5... | collective-permute-start | bytes 786440 | tf_op jit(solution)/shard_map/ppermute | solution.py:442
  68.0 8.4 %collective-permute-start.13 = (f32[4,128,128]{2,1,0:T(8,128)S(1)}, f32[4,128,128]{2,1,0:T(8,128)S(1)}, u32[]{:S(2)}, u32[]{:S(2)}) collective-permute-start(f32[4,128,128]{2,1,0:T(8,128)S(1)} %get-tuple-element.217.to_y_ref), channel_id=1, source_target_pairs={{0,16},{4,20},{8,24},{12,28},{16,0},{20,4},{24,8},{28,12},{1,17},{... | collective-permute-start | bytes 786440 | tf_op jit(solution)/shard_map/ppermute | solution.py:442
  76.7 8.4 %collective-permute-start.14 = (f32[4,128,128]{2,1,0:T(8,128)S(1)}, f32[4,128,128]{2,1,0:T(8,128)S(1)}, u32[]{:S(2)}, u32[]{:S(2)}) collective-permute-start(f32[4,128,128]{2,1,0:T(8,128)S(1)} %get-tuple-element.233), channel_id=1, source_target_pairs={{0,16},{4,20},{8,24},{12,28},{16,0},{20,4},{24,8},{28,12},{1,17},{... | collective-permute-start | bytes 786440 | tf_op jit(solution)/shard_map/ppermute | solution.py:442
  77.8 7.3 %collective-permute-start.15 = (f32[4,128,128]{2,1,0:T(8,128)S(1)}, f32[4,128,128]{2,1,0:T(8,128)S(1)}, u32[]{:S(2)}, u32[]{:S(2)}) collective-permute-start(f32[4,128,128]{2,1,0:T(8,128)S(1)} %get-tuple-element.234), channel_id=1, source_target_pairs={{0,8},{4,12},{8,0},{12,4},{16,24},{20,28},{24,16},{28,20},{1,9},{5... | collective-permute-start | bytes 786440 | tf_op jit(solution)/shard_map/ppermute | solution.py:442
  85.3 6.7 %collective-permute-start.16 = (f32[8,128,128]{2,1,0:T(8,128)S(1)}, f32[8,128,128]{2,1,0:T(8,128)S(1)}, u32[]{:S(2)}, u32[]{:S(2)}) collective-permute-start(f32[8,128,128]{2,1,0:T(8,128)S(1)} %shard_map.136.refs_0_), channel_id=1, source_target_pairs={{0,4},{4,0},{8,12},{12,8},{16,20},{20,16},{24,28},{28,24},{1,5},{5... | collective-permute-start | bytes 1572872 | tf_op jit(solution)/shard_map/ppermute | solution.py:442
